TPU v7x, 128 devices: a whole 4x4x4 slice. The times are simulated.
128 devices in a mesh: region: 16 (over x, z), orbit: 8 (over y, core).
Axes of the slice: x: 4, y: 4, z: 4, core: 2. Of those that a mesh axis runs over, the one named last changes fastest.
Arguments:
- queries: bfloat16 [8, 48, 256, 512], P('orbit', 'region'), may hold values from -24 to 24
- keys: bfloat16 [8, 16, 512, 512], P('orbit', 'region'), may hold values from -24 to 24
- values: bfloat16 [8, 16, 512, 512], P('orbit', 'region'), may hold values from -6 to 6
- block_lists: int32 [8, 48, 8], P('orbit', 'region'), may hold values from 0 to 15, as said below
- band_counts: int32 [8, 48], P('orbit', 'region'), may hold values from 4 to 8, as said below
- cotangent: bfloat16 [8, 48, 256, 1024], P('orbit', 'region'), may hold values from -6 to 6
- out_weight: bfloat16 [512, 1024], replicated, may hold values from -0.25 to 0.25
Outputs:
- layer_out: bfloat16 [8, 48, 256, 1024], P('orbit', 'region')
- d_queries: bfloat16 [8, 48, 256, 512], P('orbit', 'region')
- d_keys: bfloat16 [8, 16, 512, 512], P('orbit', 'region')
- d_values: bfloat16 [8, 16, 512, 512], P('orbit', 'region')
- d_weight: float32 [512, 1024], replicated
Inputs may be any that keep to these rules, and one draw needn't show every extreme that they name: `block_lists`: each tile's row holds 8 different band numbers; only the first band_counts entries are read. `band_counts`: tiles of the outermost regions read the most bands.
All inputs are finite; a program needn't handle non-finite values.
Results may differ from a plain program's by a relative error of at most 0.035.
Values may be sent and summed in bfloat16 or wider, within the bound.
No kernel may reach another device: no remote copies, remote signals or barrier semaphores. Data moves between devices by JAX's collectives and lax.ppermute only.
A program may use at most 192 MiB of HBM per device.

v0:
```python
import jax
import jax.numpy as jnp
from jax import lax
from jax.sharding import PartitionSpec as P

HEADS = 8
HEAD_DIM = 64


very_low = -1e30


def band_scores(query_rows, band, band_keys, scale):
    key_block = lax.dynamic_index_in_dim(band_keys, band, 0, keepdims=False)
    key_block = key_block.reshape(key_block.shape[0], HEADS, HEAD_DIM)
    scores = (
        jnp.einsum("qhd,khd->hqk", query_rows, key_block, preferred_element_type=jnp.float32)
        * scale
    )
    return (scores, key_block)


def band_probs(scores, lse, row_mask):
    return jnp.where(row_mask[None, :, None], jnp.exp(scores - lse[:, :, None]), 0.0).astype(
        jnp.bfloat16
    )


def stat_step(query_rows, row_mask, band, carry, band_keys, scale):
    running, total = carry
    scores, unused = band_scores(query_rows, band, band_keys, scale)
    masked = jnp.where(row_mask[None, :, None], scores, very_low)
    top = jnp.maximum(running, jnp.max(masked, axis=-1))
    terms = jnp.where(row_mask[None, :, None], jnp.exp(scores - top[:, :, None]), 0.0)
    return (top, total * jnp.exp(running - top) + jnp.sum(terms, axis=-1))


def value_step(query_rows, row_mask, lse, band, acc, band_keys, band_values, scale):
    scores, unused = band_scores(query_rows, band, band_keys, scale)
    probs = band_probs(scores, lse, row_mask)
    value_block = lax.dynamic_index_in_dim(band_values, band, 0, keepdims=False)
    value_block = value_block.reshape(value_block.shape[0], HEADS, HEAD_DIM)
    return acc + jnp.einsum("hqk,khd->qhd", probs, value_block, preferred_element_type=jnp.float32)


def grad_step(
    query_rows, dattn_rows, delta, row_mask, lse, band, carry, band_keys, band_values, scale
):
    dq_acc, key_grads, value_grads = carry
    scores, key_block = band_scores(query_rows, band, band_keys, scale)
    probs = band_probs(scores, lse, row_mask)
    value_block = lax.dynamic_index_in_dim(band_values, band, 0, keepdims=False)
    value_block = value_block.reshape(value_block.shape[0], HEADS, HEAD_DIM)
    d_probs = jnp.einsum(
        "qhd,khd->hqk", dattn_rows, value_block, preferred_element_type=jnp.float32
    )
    d_scores = (probs.astype(jnp.float32) * (d_probs - delta[:, :, None]) * scale).astype(
        jnp.bfloat16
    )
    dq_acc = dq_acc + jnp.einsum(
        "hqk,khd->qhd", d_scores, key_block, preferred_element_type=jnp.float32
    )
    key_part = jnp.einsum("hqk,qhd->khd", d_scores, query_rows, preferred_element_type=jnp.float32)
    value_part = jnp.einsum("hqk,qhd->khd", probs, dattn_rows, preferred_element_type=jnp.float32)
    key_grads = key_grads.at[band].add(key_part.reshape(key_part.shape[0], -1))
    value_grads = value_grads.at[band].add(value_part.reshape(value_part.shape[0], -1))
    return (dq_acc, key_grads, value_grads)


def per_device(queries, keys, values, block_lists, band_counts, cotangent, out_weight):
    scale = HEAD_DIM ** (-0.5)
    gathered_keys, gathered_values = (
        lax.all_gather(keys, "region", axis=1, tiled=True),
        lax.all_gather(values, "region", axis=1, tiled=True),
    )
    band_keys = gathered_keys[0]
    band_values = gathered_values[0]
    tiles_here = queries.shape[1]
    rows_tile = queries.shape[2]
    rows_all = tiles_here * rows_tile
    query_heads = queries[0].reshape(rows_all, HEADS, HEAD_DIM)
    lists = block_lists[0]
    counts = band_counts[0]
    full_mask = jnp.ones((rows_tile,), jnp.bool_)
    lse_parts = []
    attn_parts = []
    for tile in range(tiles_here):
        tile_rows = query_heads[tile * rows_tile : (tile + 1) * rows_tile]
        tile_ids = lists[tile]
        start = (
            jnp.full((HEADS, rows_tile), very_low, jnp.float32),
            jnp.zeros((HEADS, rows_tile), jnp.float32),
        )
        running, total = lax.fori_loop(
            0,
            counts[tile],
            lambda slot, carry: stat_step(
                tile_rows, full_mask, tile_ids[slot], carry, band_keys, scale
            ),
            start,
        )
        tile_lse = running + jnp.log(total)
        acc = lax.fori_loop(
            0,
            counts[tile],
            lambda slot, carry: value_step(
                tile_rows, full_mask, tile_lse, tile_ids[slot], carry, band_keys, band_values, scale
            ),
            jnp.zeros((rows_tile, HEADS, HEAD_DIM), jnp.float32),
        )
        lse_parts.append(tile_lse)
        attn_parts.append(acc)
    lse_all = jnp.concatenate(lse_parts, axis=1)
    attn_heads = jnp.concatenate(attn_parts, axis=0).astype(jnp.bfloat16)
    attn_flat = attn_heads.reshape(rows_all, HEADS * HEAD_DIM)
    grads_flat = cotangent[0].reshape(rows_all, cotangent.shape[3])
    layer = jnp.dot(attn_flat, out_weight, preferred_element_type=jnp.float32).astype(jnp.bfloat16)
    weight_local = jnp.einsum(
        "rh,rd->hd", attn_flat, grads_flat, preferred_element_type=jnp.float32
    )
    d_weight = lax.psum(weight_local, ("region", "orbit"))
    d_attn = jnp.einsum(
        "rd,hd->rh", grads_flat, out_weight, preferred_element_type=jnp.float32
    ).astype(jnp.bfloat16)
    dattn_heads = d_attn.reshape(rows_all, HEADS, HEAD_DIM)
    delta_all = jnp.einsum(
        "qhd,qhd->hq", attn_heads, dattn_heads, preferred_element_type=jnp.float32
    )
    zero_grads = jnp.zeros(band_keys.shape, jnp.float32)
    key_grads = zero_grads
    value_grads = zero_grads
    dq_parts = []
    for tile in range(tiles_here):
        low = tile * rows_tile
        tile_rows = query_heads[low : low + rows_tile]
        tile_dattn = dattn_heads[low : low + rows_tile]
        tile_delta = delta_all[:, low : low + rows_tile]
        tile_lse = lse_all[:, low : low + rows_tile]
        tile_ids = lists[tile]
        dq_tile, key_grads, value_grads = lax.fori_loop(
            0,
            counts[tile],
            lambda slot, carry: grad_step(
                tile_rows,
                tile_dattn,
                tile_delta,
                full_mask,
                tile_lse,
                tile_ids[slot],
                carry,
                band_keys,
                band_values,
                scale,
            ),
            (jnp.zeros((rows_tile, HEADS, HEAD_DIM), jnp.float32), key_grads, value_grads),
        )
        dq_parts.append(dq_tile)
    dq_all = jnp.concatenate(dq_parts, axis=0)
    key_sum, value_sum = (
        lax.psum_scatter(
            key_grads[None].astype(jnp.bfloat16), "region", scatter_dimension=1, tiled=True
        ).astype(jnp.float32),
        lax.psum_scatter(
            value_grads[None].astype(jnp.bfloat16), "region", scatter_dimension=1, tiled=True
        ).astype(jnp.float32),
    )
    layer_out = layer.reshape(1, tiles_here, rows_tile, layer.shape[1])
    d_queries = dq_all.astype(jnp.bfloat16).reshape(1, tiles_here, rows_tile, HEADS * HEAD_DIM)
    return (
        layer_out,
        d_queries,
        key_sum.astype(jnp.bfloat16),
        value_sum.astype(jnp.bfloat16),
        d_weight,
    )


def solution(mesh):
    return jax.shard_map(
        per_device,
        mesh=mesh,
        in_specs=(
            P("orbit", "region", None, None),
            P("orbit", "region", None, None),
            P("orbit", "region", None, None),
            P("orbit", "region", None),
            P("orbit", "region"),
            P("orbit", "region", None, None),
            P(),
        ),
        out_specs=(
            P("orbit", "region", None, None),
            P("orbit", "region", None, None),
            P("orbit", "region", None, None),
            P("orbit", "region", None, None),
            P(),
        ),
        check_vma=False,
    )
```

profile of v0, /device:TPU:0, one launch (start us, length us, event | category | flops | bytes accessed | tf_op | source)
XLA Modules:
  0.0 1027.7 jit_solution(18187602134577743568)
XLA Ops:
  10.9 72.6 %all-gather.5.cloned.1.call-done = bf16[1,16,512,512]{3,2,0,1:T(8,128)(2,1)} async-done(((bf16[1,1,512,512]{3,2,0,1:T(8,128)(2,1)}), bf16[1,16,512,512]{3,2,0,1:T(8,128)(2,1)}) %all-gather.5.cloned.1.call-update) | async-done | bytes 8388624 | tf_op jit(solution)/shard_map/all_gather | solution.py:73
  83.5 12.3 %copy.42 = bf16[16,512,512]{1,2,0:T(8,128)(2,1)} copy(bf16[16,512,512]{2,1,0:T(8,128)(2,1)} %bitcast.410) | data formatting | bytes 16777216 | tf_op jit(solution)/shard_map/while | solution.py:103
  95.8 46.5 %while.114 = (s32[]{:T(128)}, f32[8,256]{1,0:T(8,128)S(1)}, f32[8,256]{1,0:T(8,128)S(1)}, s32[]{:T(128)}, s32[8]{0:T(128)S(1)}, /*index=5*/bf16[16,512,512]{1,2,...) while((s32[]{:T(128)}, f32[8,256]{1,0:T(8,128)S(1)}, ...), condition=%wide.region_3.4_spmd, body=%wide.region_0.3_spmd.sunk | while | flops 139464704 | bytes 10330305 | solution.py:94
  142.4 13.7 %all-gather.3.cloned.1.call-done = bf16[1,16,512,512]{3,2,0,1:T(8,128)(2,1)} async-done(((bf16[1,1,512,512]{3,2,0,1:T(8,128)(2,1)}), bf16[1,16,512,512]{3,2,0,1:T(8,128)(2,1)}) %all-gather.3.cloned.1.call-update) | async-done | bytes 8388624 | tf_op jit(solution)/shard_map/all_gather | solution.py:74
  156.1 12.3 %copy.41 = bf16[16,512,512]{1,2,0:T(8,128)(2,1)} copy(bf16[16,512,512]{2,1,0:T(8,128)(2,1)} %bitcast.409) | data formatting | bytes 16777216 | tf_op jit(solution)/shard_map/while | solution.py:103
  169.3 60.7 %while.115 = (s32[]{:T(128)}, f32[256,8,64]{0,2,1:T(8,128)}, s32[]{:T(128)}, s32[8]{0:T(128)S(1)}, bf16[16,512,512]{1,2,0:T(8,128)(2,1)}, /*index=5*/bf16[16,512...) while((s32[]{:T(128)}, f32[256,8,64]{0,2,1:T(8,128)}, ...), condition=%wide.region_5.6_spmd, body=%wide.region_4.5_spmd.sunk | while | flops 271712256 | bytes 4464841 | solution.py:103
  231.7 23.9 %while.116 = (s32[]{:T(128)}, f32[8,256]{1,0:T(8,128)S(1)}, f32[8,256]{1,0:T(8,128)S(1)}, s32[]{:T(128)}, s32[8]{0:T(128)S(1)}, /*index=5*/bf16[16,512,512]{1,2,...) while((s32[]{:T(128)}, f32[8,256]{1,0:T(8,128)S(1)}, ...), condition=%wide.region_9.10_spmd, body=%wide.region_6.9_spmd.sunk | while | flops 139464704 | bytes 10330305 | solution.py:94
  256.5 30.9 %while.117 = (s32[]{:T(128)}, f32[256,8,64]{0,2,1:T(8,128)}, s32[]{:T(128)}, s32[8]{0:T(128)S(1)}, bf16[16,512,512]{1,2,0:T(8,128)(2,1)}, /*index=5*/bf16[16,512...) while((s32[]{:T(128)}, f32[256,8,64]{0,2,1:T(8,128)}, ...), condition=%wide.region_11.12_spmd, body=%wide.region_10.11_spmd.sunk | while | flops 271712256 | bytes 4464841 | solution.py:103
  289.2 29.7 %while.118 = (s32[]{:T(128)}, f32[8,256]{1,0:T(8,128)S(1)}, f32[8,256]{1,0:T(8,128)S(1)}, s32[]{:T(128)}, s32[8]{0:T(128)S(1)}, /*index=5*/bf16[16,512,512]{1,2,...) while((s32[]{:T(128)}, f32[8,256]{1,0:T(8,128)S(1)}, ...), condition=%wide.region_15.16_spmd, body=%wide.region_12.15_spmd.sunk | while | flops 139464704 | bytes 10330305 | solution.py:94
  319.7 37.4 %while.119 = (s32[]{:T(128)}, f32[256,8,64]{0,2,1:T(8,128)}, s32[]{:T(128)}, s32[8]{0:T(128)S(1)}, bf16[16,512,512]{1,2,0:T(8,128)(2,1)}, /*index=5*/bf16[16,512...) while((s32[]{:T(128)}, f32[256,8,64]{0,2,1:T(8,128)}, ...), condition=%wide.region_17.18_spmd, body=%wide.region_16.17_spmd.sunk | while | flops 271712256 | bytes 4464841 | solution.py:103
  361.5 7.9 broadcast_in_dim.75
  369.4 7.9 broadcast_in_dim.75.clone
  377.3 109.9 %while.120 = (s32[]{:T(128)}, f32[256,8,64]{0,2,1:T(8,128)S(1)}, f32[16,512,512]{1,2,0:T(8,128)}, f32[16,512,512]{1,2,0:T(8,128)}, s32[]{:T(128)}, /*index=5*/s3...) while((s32[]{:T(128)}, f32[256,8,64]{0,2,1:T(8,128)S(1)}, ...), condition=%wide.region_20.21_spmd, body=%wide.region_18.20_spmd.sunk | while | flops 680656896 | bytes 26756368 | solution.py:140
  487.3 56.6 %while.121 = (s32[]{:T(128)}, f32[256,8,64]{0,2,1:T(8,128)S(1)}, f32[16,512,512]{1,2,0:T(8,128)}, f32[16,512,512]{1,2,0:T(8,128)}, s32[]{:T(128)}, /*index=5*/s3...) while((s32[]{:T(128)}, f32[256,8,64]{0,2,1:T(8,128)S(1)}, ...), condition=%wide.region_23.24_spmd, body=%wide.region_21.0_spmd.sunk | while | flops 680656896 | bytes 27804972 | solution.py:140
  547.4 71.8 %while.122 = (s32[]{:T(128)}, f32[256,8,64]{0,2,1:T(8,128)S(1)}, f32[16,512,512]{1,2,0:T(8,128)}, f32[16,512,512]{1,2,0:T(8,128)}, s32[]{:T(128)}, /*index=5*/s3...) while((s32[]{:T(128)}, f32[256,8,64]{0,2,1:T(8,128)S(1)}, ...), condition=%wide.region_26.27_spmd, body=%wide.region_24.0_spmd.sunk | while | flops 680656896 | bytes 27804972 | solution.py:140
  557.2 4.2 fusion.215
  571.4 4.1 fusion.215
  585.6 4.1 fusion.215
  599.8 4.1 fusion.215
  619.1 13.9 %copy.57 = bf16[16,512,512]{2,1,0:T(8,128)(2,1)} copy(f32[16,512,512]{1,2,0:T(8,128)} %get-tuple-element.534) | data formatting | bytes 25165824 | tf_op jit(solution)/shard_map/while | solution.py:140
  633.1 13.9 %copy.58 = bf16[16,512,512]{2,1,0:T(8,128)(2,1)} copy(f32[16,512,512]{1,2,0:T(8,128)} %get-tuple-element.535) | data formatting | bytes 25165824 | tf_op jit(solution)/shard_map/while | solution.py:140
  652.9 189.7 %all-reduce.4.cloned.1.call-done = f32[512,1024]{1,0:T(8,128)} async-done(((f32[512,1024]{1,0:T(8,128)}), f32[512,1024]{1,0:T(8,128)}) %all-reduce.4.cloned.1.call-update) | async-done | bytes 2097168 | tf_op jit(solution)/shard_map/psum | solution.py:121
  842.5 87.3 %reduce-scatter.13.cloned.1.call-done = bf16[1,1,512,512]{3,2,1,0:T(8,128)(2,1)} async-done(((bf16[1,16,512,512]{3,2,1,0:T(8,128)(2,1)}), bf16[1,1,512,512]{3,2,1,0:T(8,128)(2,1)}) %reduce-scatter.13.cloned.1.call-update) | async-done | bytes 524304
  929.9 88.1 %reduce-scatter.15.cloned.1.call-done = bf16[1,1,512,512]{3,2,1,0:T(8,128)(2,1)} async-done(((bf16[1,16,512,512]{3,2,1,0:T(8,128)(2,1)}), bf16[1,1,512,512]{3,2,1,0:T(8,128)(2,1)}) %reduce-scatter.15.cloned.1.call-update) | async-done | bytes 524304
  (410 shorter events, 341.7 us)
Async XLA Ops:
  7.2 351.0 %copy-start = (bf16[1,3,256,1024]{3,2,1,0:T(8,128)(2,1)S(1)}, bf16[1,3,256,1024]{3,2,1,0:T(8,128)(2,1)}, u32[]{:S(2)}) copy-start(bf16[1,3,256,1024]{3,2,1,0:T(8,128)(2,1)} %param.42) | copy-start | bytes 4718596
  7.2 3.1 copy-start.5
  7.2 3.7 copy-start.6
  7.2 76.3 %all-gather.5.cloned.1.call-start = ((), (), s32[]{:S(2)}) async-start(), calls=%async_computation.3 | async-start | bytes 8912896 | tf_op jit(solution)/shard_map/all_gather | solution.py:73
  7.9 148.2 %all-gather.3.cloned.1.call-start = ((), (), s32[]{:S(2)}) async-start(), calls=%async_computation.2 | async-start | bytes 8912896 | tf_op jit(solution)/shard_map/all_gather | solution.py:74
  8.7 833.8 %all-reduce.4.cloned.1.call-start = ((), (), s32[]{:S(2)}) async-start(), calls=%async_computation.4 | async-start | bytes 4194304 | tf_op jit(solution)/shard_map/psum | solution.py:121
  358.1 2.5 copy-start.3
  369.4 7.9 copy-start.4
  487.9 5.7 copy-start.2
  501.9 5.7 copy-start.2
  515.8 5.7 copy-start.2
  529.8 5.7 copy-start.2
  547.3 382.6 %reduce-scatter.13.cloned.1.call-start = ((), (), s32[]{:S(2)}) async-start(), calls=%async_computation.5 | async-start | bytes 8912896
  550.8 3.2 copy-start.1
  565.0 3.2 copy-start.1
  579.2 3.2 copy-start.1
  593.4 3.2 copy-start.1
  607.5 3.2 copy-start.1
  633.1 384.9 %reduce-scatter.15.cloned.1.call-start = ((), (), s32[]{:S(2)}) async-start(), calls=%async_computation.6 | async-start | bytes 8912896
Sparse Core Ops, SparseCore 0:
  10.2 73.3 all-gather.4
  85.7 70.4 all-gather.2
  547.4 295.0 all-reduce.3
  846.4 83.4 reduce-scatter.12
  933.7 84.2 reduce-scatter.14
where the time goes:
time: 1040 us; the launch traced here: 1030 us
  waiting for transfers between devices  453 us (44%)
  local copies, waits for them, and re-layouts  186 us (18%)
  matrix products  142 us (14%)
  loops' own time  136 us (13%)
  other arithmetic  97 us (9%)
  between operations  14 us (1%)
    psum x1, waiting for transfers between devices, per_device(): d_weight = lax.psum(weight_local, ('region', 'orbit'))  190 us
    unnamed x7, waiting for transfers between devices  177 us
    all_gather x1, waiting for transfers between devices, per_device(): lax.all_gather(keys, 'region', axis=1, tiled=True)  72.6 us
    scatter-add x17, other arithmetic, grad_step(): key_grads = key_grads.at[band].add(key_part.reshape(key_part.shape[0], -1))  68.3 us
    dynamic_slice x51, local copies, waits for them, and re-layouts, band_scores(): key_block = lax.dynamic_index_in_dim(band_keys, band, 0, keepdims=False)  58.6 us
    dot_general x17, matrix products, value_step(): jnp.einsum('hqk,khd->qhd', probs, value_block, preferred_element_type=jnp...  52.6 us
    another operation x3, loops' own time, per_device(): lax.fori_loop(0, counts[tile], lambda slot, carry: stat_step(tile_rows, f...  46.4 us
    another operation x3, loops' own time, per_device(): lax.fori_loop(0, counts[tile], lambda slot, carry: grad_step(tile_rows, t...  44.9 us
  transfers between devices with their start and end apart: 5, of which 5 were waited for; matrix products, arithmetic and copies ran while one was open for 13% of the time, Pallas kernels for 0%

commit v1 on v0

v1 whole, which is shorter than its diff:
```python
import functools

import jax
import jax.numpy as jnp
from jax import lax
from jax.experimental import pallas as pl
from jax.experimental.pallas import tpu as pltpu
from jax.sharding import PartitionSpec as P

HEADS = 8
HEAD_DIM = 64
BANDS = 16
BT = 512
QROWS = 256
HALF = 128
TILES_DEV = 3
TILES = 48
MAXB = 8
D = 1024
HW = 512
CHUNKS = 2
PAIRS = 208
SCALE = HEAD_DIM**-0.5
LOW = -1e30
BF16 = jnp.bfloat16
F32 = jnp.float32

NT = (((1,), (1,)), ((), ()))


def dot(a, b, dims=(((1,), (0,)), ((), ()))):
    return lax.dot_general(a, b, dims, preferred_element_type=F32)


def params(mib=56):
    return pltpu.CompilerParams(vmem_limit_bytes=mib << 20)


def cost(flops, nbytes, exps=0):
    return pl.CostEstimate(flops=int(flops), bytes_accessed=int(nbytes), transcendentals=int(exps))


VMEM = pl.BlockSpec(memory_space=pltpu.VMEM)
SMEM = pl.BlockSpec(memory_space=pltpu.SMEM)


def pack_body(q_ref, k_ref, v_ref, out_ref):
    kt = k_ref[...].T
    vt = v_ref[...].T
    qt = (q_ref[...].astype(F32) * SCALE).astype(BF16).T
    for head in range(2):
        rows = slice(head * 64, head * 64 + 64)
        for half in range(2):
            dest = 2 * head + half
            for j in range(4):
                lanes = slice(j * 128, j * 128 + 128)
                out_ref[dest, j * 128 : j * 128 + 64, :] = kt[rows, lanes]
                out_ref[dest, j * 128 + 64 : j * 128 + 128, :] = vt[rows, lanes]
            for t in range(TILES_DEV):
                low = t * QROWS + half * HALF
                out_ref[dest, BT + t * 64 : BT + t * 64 + 64, :] = qt[rows, low : low + HALF]


def pack(q, k, v):
    rows = BT + TILES_DEV * 64
    return pl.pallas_call(
        pack_body,
        grid=(4,),
        in_specs=[
            pl.BlockSpec((TILES_DEV * QROWS, 128), lambda p: (0, p)),
            pl.BlockSpec((BT, 128), lambda p: (0, p)),
            pl.BlockSpec((BT, 128), lambda p: (0, p)),
        ],
        out_specs=pl.BlockSpec((4, rows, 128), lambda p: (p, 0, 0)),
        out_shape=jax.ShapeDtypeStruct((16, rows, 128), BF16),
        compiler_params=params(24),
        cost_estimate=cost(0, 8e6),
        name="pack",
    )(q, k, v)


def dattn_body(w_ref, g_ref, out_ref):
    dt = dot(w_ref[...], g_ref[...], NT).astype(BF16)
    for head in range(2):
        for half in range(2):
            for t in range(TILES_DEV):
                low = t * QROWS + half * HALF
                out_ref[2 * head + half, t * 64 : t * 64 + 64, :] = dt[
                    head * 64 : head * 64 + 64, low : low + HALF
                ]


def dattn(w, g):
    rows = TILES_DEV * QROWS
    return pl.pallas_call(
        dattn_body,
        grid=(4,),
        in_specs=[
            pl.BlockSpec((128, D), lambda p: (p, 0)),
            pl.BlockSpec((rows, D), lambda p: (0, 0)),
        ],
        out_specs=pl.BlockSpec((4, TILES_DEV * 64, 128), lambda p: (p, 0, 0)),
        out_shape=jax.ShapeDtypeStruct((16, TILES_DEV * 64, 128), BF16),
        compiler_params=params(24),
        cost_estimate=cost(2 * rows * D * HW, 4e6),
        name="dattn",
    )(w, g)


def plan_of(lists, counts):
    slots = jnp.arange(MAXB)[None, :] < counts[:, None]
    member = (
        (lists[:, :, None] == jnp.arange(BANDS)[None, None, :]) & slots[:, :, None]
    ).any(axis=1)
    member = member.T.astype(jnp.int32)
    place = jnp.cumsum(member, axis=1) - member
    size = (member.sum(axis=1) + 1) // 2
    base = jnp.cumsum(size) - size
    flat = jnp.where(member > 0, 2 * base[:, None] + place, -1)
    hit = flat[None] == jnp.arange(2 * PAIRS)[:, None, None]
    tile = jnp.arange(TILES)[None, None, :]
    band = jnp.arange(BANDS)[None, :, None]
    code = jnp.sum(jnp.where(hit, band * 64 + tile + 1, 0), axis=(1, 2)).reshape(PAIRS, 2)
    who = jnp.where(code > 0, (code & 63) - 1, TILES)
    number = (size.sum() + 1) // 2
    return jnp.stack(
        [who[:, 0], who[:, 1], code[:, 0] >> 6, jnp.full((PAIRS,), number, jnp.int32)]
    ).astype(jnp.int32)


def forward_body(plan, recv, attn_ref, lse_ref, kv_ref, kt_ref, qt_ref, vt, top, total, acc, s0, s1):
    def unpack_band(b, carry):
        kvt = jnp.concatenate([recv[b, j * 128 : j * 128 + 128, :] for j in range(4)], axis=1)
        kv_ref[b] = kvt.T
        kt_ref[b] = kvt[:64]
        vt[b] = kvt[64:]
        for t in range(TILES_DEV):
            qt_ref[b * TILES_DEV + t] = recv[b, BT + t * 64 : BT + t * 64 + 64, :]
        return carry

    lax.fori_loop(0, BANDS, unpack_band, 0)
    qt_ref[TILES] = jnp.zeros((64, HALF), BF16)
    top[...] = jnp.full(top.shape, LOW, F32)
    total[...] = jnp.zeros(total.shape, F32)
    acc[...] = jnp.zeros(acc.shape, F32)
    blank = jnp.zeros((64, 2 * HALF), BF16)

    def scores(i, dst):
        w = jnp.concatenate([qt_ref[plan[0, i]], qt_ref[plan[1, i]]], axis=1)
        dst[...] = dot(kv_ref[plan[2, i]], jnp.concatenate([w, blank], axis=0))

    def absorb(i, src):
        a, c, b = plan[0, i], plan[1, i], plan[2, i]
        old = jnp.concatenate([top[a], top[c]], axis=1)
        new = jnp.maximum(old, jnp.max(src[...], axis=0, keepdims=True))
        fade = jnp.exp(old - new)
        p = jnp.exp(src[...] - new)
        part = jnp.sum(p, axis=0, keepdims=True)
        o = dot(vt[b], p.astype(BF16))
        for x, lanes in ((a, slice(0, HALF)), (c, slice(HALF, 2 * HALF))):
            top[x] = new[:, lanes]
            total[x] = total[x] * fade[:, lanes] + part[:, lanes]
            acc[x] = acc[x] * fade[:, lanes] + o[:, lanes]

    scores(0, s0)

    def two(j, carry):
        scores(2 * j + 1, s1)
        absorb(2 * j, s0)
        scores(2 * j + 2, s0)
        absorb(2 * j + 1, s1)
        return carry

    lax.fori_loop(0, plan[3, 0], two, 0)

    def finish(x, carry):
        attn_ref[x] = (acc[x] / total[x]).astype(BF16)
        lse_ref[x] = top[x] + jnp.log(total[x])
        return carry

    lax.fori_loop(0, TILES, finish, 0)
    lse_ref[TILES] = jnp.full((1, HALF), -LOW, F32)


def forward(plan, recv):
    return pl.pallas_call(
        forward_body,
        in_specs=[SMEM, VMEM],
        out_specs=[VMEM] * 5,
        out_shape=[
            jax.ShapeDtypeStruct((TILES, 64, HALF), BF16),
            jax.ShapeDtypeStruct((TILES + 1, 1, HALF), F32),
            jax.ShapeDtypeStruct((BANDS, BT, 128), BF16),
            jax.ShapeDtypeStruct((BANDS, 64, BT), BF16),
            jax.ShapeDtypeStruct((TILES + 1, 64, HALF), BF16),
        ],
        scratch_shapes=[
            pltpu.VMEM((BANDS, 64, BT), BF16),
            pltpu.VMEM((TILES + 1, 1, HALF), F32),
            pltpu.VMEM((TILES + 1, 1, HALF), F32),
            pltpu.VMEM((TILES + 1, 64, HALF), F32),
            pltpu.VMEM((BT, 2 * HALF), F32),
            pltpu.VMEM((BT, 2 * HALF), F32),
        ],
        compiler_params=params(40),
        cost_estimate=cost(2.4e10, 2e7, 16e6),
        name="forward",
    )(plan, recv)


def backward_body(last, plan, kv, kt, qt, dot_, attn, lse, dq_in, dkv_ref, dq_ref, w1, delta, dkv, dq, a0, c0, a1, c1):
    rows = kv.shape[1]

    def prepare(x, carry):
        blank = jnp.zeros((64, HALF), BF16)
        w1[x] = jnp.concatenate(
            [jnp.concatenate([qt[x], blank], axis=1), jnp.concatenate([blank, dot_[x]], axis=1)], axis=0
        )
        delta[x] = jnp.sum(attn[x].astype(F32) * dot_[x].astype(F32), axis=0, keepdims=True)
        return carry

    lax.fori_loop(0, TILES, prepare, 0)
    w1[TILES] = jnp.zeros((128, 2 * HALF), BF16)
    delta[TILES] = jnp.zeros((1, HALF), F32)
    dkv[...] = jnp.zeros(dkv.shape, F32)
    if dq_in is None:
        dq[...] = jnp.zeros(dq.shape, F32)
    else:
        dq[...] = dq_in[...]

    def scores(i, dst_a, dst_c):
        band = kv[plan[2, i]]
        dst_a[...] = dot(band, w1[plan[0, i]])
        dst_c[...] = dot(band, w1[plan[1, i]])

    def absorb(i, src_a, src_c):
        a, c, b = plan[0, i], plan[1, i], plan[2, i]
        both = []
        for x, src in ((a, src_a), (c, src_c)):
            p = jnp.exp(src[:, :HALF] - lse[x])
            ds = p * (src[:, HALF:] - delta[x])
            both.append((ds.astype(BF16), p.astype(BF16)))
        (ds_a, p_a), (ds_c, p_c) = both
        dkv[b] += dot(
            jnp.concatenate([ds_a, p_a, ds_c, p_c], axis=1),
            jnp.concatenate([w1[a], w1[c]], axis=1),
            NT,
        )
        part = dot(kt[b], jnp.concatenate([ds_a, ds_c], axis=1))
        dq[a] += part[:, :HALF]
        dq[c] += part[:, HALF:]

    scores(0, a0, c0)

    def two(j, carry):
        scores(2 * j + 1, a1, c1)
        absorb(2 * j, a0, c0)
        scores(2 * j + 2, a0, c0)
        absorb(2 * j + 1, a1, c1)
        return carry

    lax.fori_loop(0, plan[3, 0], two, 0)

    def finish(b, carry):
        dkv_ref[b] = dkv[b].astype(BF16)
        return carry

    lax.fori_loop(0, BANDS, finish, 0)
    if last:

        def finish_q(x, carry):
            dq_ref[x] = (dq[x] * SCALE).astype(BF16)
            return carry

        lax.fori_loop(0, TILES, finish_q, 0)
    else:
        dq_ref[...] = dq[...]


def backward(chunk, plan, kv, kt, qt, dot_, attn, lse, dq_in):
    rows = BT // CHUNKS
    last = chunk == CHUNKS - 1
    first = dq_in is None
    body = functools.partial(backward_body, last)
    if first:
        inner = body

        def body(plan, kv, kt, qt, dot_, attn, lse, *rest):
            return inner(plan, kv, kt, qt, dot_, attn, lse, None, *rest)

    specs = [
        SMEM,
        pl.BlockSpec((BANDS, rows, 128), lambda i: (0, chunk, 0)),
        pl.BlockSpec((BANDS, 64, rows), lambda i: (0, 0, chunk)),
        VMEM,
        VMEM,
        VMEM,
        VMEM,
    ]
    args = [plan, kv, kt, qt, dot_, attn, lse]
    if not first:
        specs.append(VMEM)
        args.append(dq_in)
    dq_shape = (
        jax.ShapeDtypeStruct((TILES, 64, HALF), BF16)
        if last
        else jax.ShapeDtypeStruct((TILES + 1, 64, HALF), F32)
    )
    return pl.pallas_call(
        body,
        grid=(1,),
        in_specs=specs,
        out_specs=[VMEM, VMEM],
        out_shape=[jax.ShapeDtypeStruct((BANDS, rows, 128), BF16), dq_shape],
        scratch_shapes=[
            pltpu.VMEM((TILES + 1, 128, 2 * HALF), BF16),
            pltpu.VMEM((TILES + 1, 1, HALF), F32),
            pltpu.VMEM((BANDS, rows, 128), F32),
            pltpu.VMEM((TILES + 1, 64, HALF), F32),
        ]
        + [pltpu.VMEM((rows, 2 * HALF), F32)] * 4,
        compiler_params=params(40),
        cost_estimate=cost(5e10 / CHUNKS, 2e7, 16e6 / CHUNKS),
        name="backward",
    )(*args)


def project_body(recv, w_ref, g_ref, layer_ref, dw_ref, acc):
    t = pl.program_id(0)
    low = pl.multiple_of(t * 64, 64)
    heads = [
        jnp.concatenate([recv[2 * h, pl.ds(low, 64), :], recv[2 * h + 1, pl.ds(low, 64), :]], axis=1)
        for h in range(HEADS)
    ]
    attn_t = jnp.concatenate(heads, axis=0)
    layer_ref[...] = dot(attn_t.T, w_ref[...]).astype(BF16)
    term = dot(attn_t, g_ref[...])

    @pl.when(t == 0)
    def _():
        acc[...] = term

    @pl.when(t > 0)
    def _():
        acc[...] += term

    @pl.when(t == TILES_DEV - 1)
    def _():
        dw_ref[...] = acc[...].astype(BF16)


def project(recv, w, g):
    rows = TILES_DEV * QROWS
    return pl.pallas_call(
        project_body,
        grid=(TILES_DEV,),
        in_specs=[
            pl.BlockSpec((16, TILES_DEV * 64, 128), lambda t: (0, 0, 0)),
            pl.BlockSpec((HW, D), lambda t: (0, 0)),
            pl.BlockSpec((QROWS, D), lambda t: (t, 0)),
        ],
        out_specs=[
            pl.BlockSpec((QROWS, D), lambda t: (t, 0)),
            pl.BlockSpec((HW, D), lambda t: (0, 0)),
        ],
        out_shape=[jax.ShapeDtypeStruct((rows, D), BF16), jax.ShapeDtypeStruct((HW, D), BF16)],
        scratch_shapes=[pltpu.VMEM((HW, D), F32)],
        compiler_params=params(40),
        cost_estimate=cost(4 * rows * D * HW, 8e6),
        name="project",
    )(recv, w, g)


def unpack_body(*refs):
    dq_in, parts = refs[0], refs[1 : 1 + CHUNKS]
    dq_ref, dk_ref, dv_ref = refs[1 + CHUNKS :]
    heads = []
    for head in range(2):
        blocks = []
        for t in range(TILES_DEV):
            for half in range(2):
                blocks.append(dq_in[2 * head + half, t * 64 : t * 64 + 64, :])
        heads.append(jnp.concatenate(blocks, axis=1))
    dq_ref[...] = jnp.concatenate(heads, axis=0).T
    rows = BT // CHUNKS
    left = lax.broadcasted_iota(jnp.int32, (rows, 128), 1) < 64
    for chunk in range(CHUNKS):
        part = parts[chunk]
        x = part[0].astype(F32) + part[1].astype(F32)
        y = part[2].astype(F32) + part[3].astype(F32)
        at = slice(chunk * rows, chunk * rows + rows)
        dk_ref[at, :] = jnp.where(left, x, pltpu.roll(y, 64, 1)).astype(BF16)
        dv_ref[at, :] = jnp.where(left, pltpu.roll(x, 64, 1), y).astype(BF16)


def unpack(dq, parts):
    rows = TILES_DEV * QROWS
    return pl.pallas_call(
        unpack_body,
        grid=(4,),
        in_specs=[pl.BlockSpec((4, TILES_DEV * 64, 128), lambda p: (p, 0, 0))]
        + [pl.BlockSpec((4, BT // CHUNKS, 128), lambda p: (p, 0, 0))] * CHUNKS,
        out_specs=[
            pl.BlockSpec((rows, 128), lambda p: (0, p)),
            pl.BlockSpec((BT, 128), lambda p: (0, p)),
            pl.BlockSpec((BT, 128), lambda p: (0, p)),
        ],
        out_shape=[
            jax.ShapeDtypeStruct((rows, HW), BF16),
            jax.ShapeDtypeStruct((BT, HW), BF16),
            jax.ShapeDtypeStruct((BT, HW), BF16),
        ],
        compiler_params=params(24),
        cost_estimate=cost(0, 8e6),
        name="unpack",
    )(dq, *parts)


def swap(x, axes="region"):
    return lax.all_to_all(x, axes, 0, 0, tiled=True)


def per_device(devices, queries, keys, values, block_lists, band_counts, cotangent, out_weight):
    rows = TILES_DEV * QROWS
    q, g = queries.reshape(rows, HW), cotangent.reshape(rows, D)
    recv1 = swap(pack(q, keys.reshape(BT, HW), values.reshape(BT, HW)))
    recv2 = swap(dattn(out_weight, g)).reshape(TILES, 64, HALF)
    where = jnp.concatenate([block_lists[0], band_counts[0][:, None]], axis=1)
    where = lax.all_gather(where, "region", axis=0, tiled=True)
    plan = plan_of(where[:, :MAXB], where[:, MAXB])

    attn, lse, kv, kt, qt = forward(plan, recv1)
    recv3 = swap(attn.reshape(16, TILES_DEV * 64, HALF))
    dq = None
    parts = []
    for chunk in range(CHUNKS):
        part, dq = backward(chunk, plan, kv, kt, qt, recv2, attn, lse, dq)
        parts.append(swap(part))
    layer, dw = project(recv3, out_weight, g)
    dw = swap(dw.reshape(devices, HW // devices, D), ("region", "orbit"))
    dw = jnp.sum(dw.astype(F32), axis=0, keepdims=True).astype(BF16)
    dw = swap(jnp.broadcast_to(dw, (devices, HW // devices, D)), ("region", "orbit"))
    d_weight = dw.reshape(HW, D).astype(F32)
    dq = swap(dq.reshape(16, TILES_DEV * 64, HALF))
    d_q, d_k, d_v = unpack(dq, parts)
    return (
        layer.reshape(1, TILES_DEV, QROWS, D),
        d_q.reshape(1, TILES_DEV, QROWS, HW),
        d_k.reshape(1, 1, BT, HW),
        d_v.reshape(1, 1, BT, HW),
        d_weight,
    )


def solution(mesh):
    four = P("orbit", "region", None, None)
    return jax.shard_map(
        functools.partial(per_device, mesh.devices.size),
        mesh=mesh,
        in_specs=(four, four, four, P("orbit", "region", None), P("orbit", "region"), four, P()),
        out_specs=(four, four, four, four, P()),
        check_vma=False,
    )
```

time: 1040 us -> 334 us (0.32); the launches traced: 1030 us -> 335 us
  waiting for transfers between devices: 453 us -> 36.6 us
  local copies, waits for them, and re-layouts: 186 us -> 25.5 us
  matrix products: 142 us -> 0 us
  loops' own time: 136 us -> 0 us
  blocking collectives: 0 us -> 129 us
  Pallas kernels: 0 us -> 112 us
  other arithmetic: 97 us -> 3.51 us
  starting transfers between devices: 0.2 us -> 26.9 us
  between operations: 14 us -> 1.53 us
    psum x1 -> x0, waiting for transfers between devices: 190 us -> none  [per_device(): d_weight = lax.psum(weight_local, ('region', 'orbit'))]
    unnamed x7 -> x0, waiting for transfers between devices: 177 us -> none
    dot_general x122 -> x0, matrix products: 142 us -> none  [the longest x17 52.6 us: value_step(): jnp.einsum('hqk,khd->qhd', probs, value_block, preferred_element_type=jnp...]
    another operation x9 -> x0, loops' own time: 136 us -> none  [the longest x3 46.4 us: per_device(): lax.fori_loop(0, counts[tile], lambda slot, carry: stat_step(tile_rows, f...]
    pallas_call x0 -> x7, Pallas kernels: none -> 112 us  [the longest x2 63.4 us: backward(): pl.pallas_call(body, grid=(1,), in_specs=specs, out_specs=[VMEM, VMEM], o...]
    dynamic_slice x119 -> x0, local copies, waits for them, and re-layouts: 107 us -> none  [the longest x51 58.6 us: band_scores(): key_block = lax.dynamic_index_in_dim(band_keys, band, 0, keepdims=False)]
    all_gather x2 -> x0, waiting for transfers between devices: 86.4 us -> none  [the longest x1 72.6 us: per_device(): lax.all_gather(keys, 'region', axis=1, tiled=True)]
    all_to_all x0 -> x3, blocking collectives: none -> 74.2 us  [swap(): return lax.all_to_all(x, axes, 0, 0, tiled=True)]
  transfers between devices with their start and end apart: 5 -> 5, of which waited for: 5 -> 3; matrix products, arithmetic and copies ran while one was open for 13% -> 2% of each run, Pallas kernels for 0% -> 14%
where the time goes in v1:
time: 334 us; the launch traced here: 335 us
  blocking collectives  129 us (39%)
  Pallas kernels  112 us (34%)
  waiting for transfers between devices  36.6 us (11%)
  starting transfers between devices  26.9 us (8%)
  local copies, waits for them, and re-layouts  25.5 us (8%)
  other arithmetic  3.51 us (1%)
    all_to_all x3, blocking collectives, swap(): return lax.all_to_all(x, axes, 0, 0, tiled=True)  74.2 us
    pallas_call x2, Pallas kernels, backward(): pl.pallas_call(body, grid=(1,), in_specs=specs, out_specs=[VMEM, VMEM], o...  63.4 us
    all_gather x1, blocking collectives, per_device(): where = lax.all_gather(where, 'region', axis=0, tiled=True)  54.7 us
    pallas_call x1, Pallas kernels, forward(): pl.pallas_call(forward_body, in_specs=[SMEM, VMEM], out_specs=[VMEM] * 5,...  37.2 us
    all_to_all x5, waiting for transfers between devices, swap(): return lax.all_to_all(x, axes, 0, 0, tiled=True)  36.6 us
    all_to_all x5, starting transfers between devices, swap(): return lax.all_to_all(x, axes, 0, 0, tiled=True)  26.9 us
    unnamed x48, local copies, waits for them, and re-layouts  19.5 us
  transfers between devices with their start and end apart: 5, of which 3 were waited for; matrix products, arithmetic and copies ran while one was open for 2% of the time, Pallas kernels for 14%

profile of v1, /device:TPU:0, one launch (start us, length us, event | category | flops | bytes accessed | tf_op | source)
XLA Modules:
  0.0 335.0 jit_solution(11710065533058145511)
XLA Ops:
  3.9 2.6 pack.1
  6.4 8.1 %all-to-all-start = ((bf16[16,704,128]{2,1,0:T(8,128)(2,1)}), bf16[16,704,128]{2,1,0:T(8,128)(2,1)S(1)}, u32[]{:S(2)}, u32[]{:S(2)}) async-start(bf16[16,704,128]{2,1,0:T(8,128)(2,1)} %pack.1), calls=%async_computation | async-start | bytes 5767168 | tf_op jit(solution)/shard_map/all_to_all | solution.py:420
  14.7 54.7 %all-gather = s32[16,3,9]{2,1,0:T(4,128)S(1)} all-gather(s32[1,3,9]{2,1,0:T(4,128)S(1)} %add_bitcast_fusion), channel_id=1, replica_groups=mesh['region'=16,'orbit'=8] {'region'}, dimensions={0}, use_global_device_ids=true | all-gather | bytes 1836 | tf_op jit(solution)/shard_map/all_gather | solution.py:429
  72.2 1.4 copy-done
  74.8 3.3 dattn.1
  78.5 5.7 %all-to-all-start.2 = ((bf16[16,192,128]{2,1,0:T(8,128)(2,1)}), bf16[16,192,128]{2,1,0:T(8,128)(2,1)}, u32[]{:S(2)}, u32[]{:S(2)}) async-start(bf16[16,192,128]{2,1,0:T(8,128)(2,1)} %dattn.1), calls=%async_computation.2 | async-start | bytes 1572864 | tf_op jit(solution)/shard_map/all_to_all | solution.py:420
  84.3 37.2 %forward.1 = (bf16[48,64,128]{2,1,0:T(8,128)(2,1)S(1)}, f32[49,1,128]{2,1,0:T(1,128)S(1)}, bf16[16,512,128]{2,1,0:T(8,128)(2,1)S(1)}, bf16[16,64,512]{2,1,0:T(8,128)(2,1)S(1)}, bf16[49,64,128]{2,1,0:T(8,128)(2,1)S(1)}) custom-call(s32[4,208]{1,0:T(4,128)S(1)} %add_add_fusion.1.plan, bf16[16,704,128]{2,1,0:T(8,128)(2,1)S(1)} %all-to-all-done.recv), custom_call_target="tpu_custom_call" | custom-call | flops 24000000000 | bytes 20000000 | tf_op jit(solution)/shard_map/forward/pallas_call | solution.py:186
  126.7 1.6 copy-done.15
  130.7 31.6 %backward.2 = (bf16[16,256,128]{2,1,0:T(8,128)(2,1)S(1)}, f32[49,64,128]{2,1,0:T(8,128)S(1)}) custom-call(s32[4,208]{1,0:T(4,128)S(1)} %add_add_fusion.1.plan, bf16[16,512,128]{2,1,0:T(8,128)(2,1)S(1)} %copy-done.15, bf16[16,64,512]{2,1,0:T(8,128)(2,1)S(1)} %copy-done.18, bf16[49,64,128]{2,1,0:T(8,128)(2,1)S(1)} %copy-done.20, ...), custom_call_target="tpu_custom_call" | custom-call | flops 24999999488 | bytes 20000000 | tf_op jit(solution)/shard_map/backward/pallas_call | solution.py:309
  163.3 31.8 %backward.3 = (bf16[16,256,128]{2,1,0:T(8,128)(2,1)S(1)}, bf16[48,64,128]{2,1,0:T(8,128)(2,1)S(1)}) custom-call(s32[4,208]{1,0:T(4,128)S(1)} %add_add_fusion.1.plan, bf16[16,512,128]{2,1,0:T(8,128)(2,1)S(1)} %copy-done.16, bf16[16,64,512]{2,1,0:T(8,128)(2,1)S(1)} %copy-done.18, bf16[49,64,128]{2,1,0:T(8,128)(2,1)S(1)} %copy-done.20, ...), custom_call_target="tpu_custom_call" | custom-call | flops 24999999488 | bytes 20000000 | tf_op jit(solution)/shard_map/backward/pallas_call | solution.py:309
  195.1 18.3 %all_to_all.40.refs_0_ = bf16[16,192,128]{2,1,0:T(8,128)(2,1)S(1)} all-to-all(bf16[16,192,128]{2,1,0:T(8,128)(2,1)S(1)} %bitcast.38), channel_id=1, replica_groups=mesh['region'=16,'orbit'=8] {'region'}, dimensions={0} | all-to-all | bytes 1572864 | tf_op jit(solution)/shard_map/all_to_all | solution.py:420
  213.4 15.0 %all_to_all.41.recv = bf16[16,192,128]{2,1,0:T(8,128)(2,1)} all-to-all(bf16[16,192,128]{2,1,0:T(8,128)(2,1)S(1)} %bitcast.37), channel_id=1, replica_groups=mesh['region'=16,'orbit'=8] {'region'}, dimensions={0} | all-to-all | bytes 1572864 | tf_op jit(solution)/shard_map/all_to_all | solution.py:420
  228.4 3.7 %all-to-all-start.5 = ((bf16[16,256,128]{2,1,0:T(8,128)(2,1)}), bf16[16,256,128]{2,1,0:T(8,128)(2,1)S(1)}, u32[]{:S(2)}, u32[]{:S(2)}) async-start(bf16[16,256,128]{2,1,0:T(8,128)(2,1)} %copy-done.5), calls=%async_computation.5 | async-start | bytes 2097152 | tf_op jit(solution)/shard_map/all_to_all | solution.py:420
  234.6 3.6 %project.1 = (bf16[768,1024]{1,0:T(8,128)(2,1)}, bf16[512,1024]{1,0:T(8,128)(2,1)S(1)}) custom-call(bf16[16,192,128]{2,1,0:T(8,128)(2,1)S(1)} %copy-done.11, bf16[512,1024]{1,0:T(8,128)(2,1)S(1)} %copy-done.3, bf16[768,1024]{1,0:T(8,128)(2,1)S(1)} %bitcast.35), custom_call_target="tpu_custom_call" | custom-call | flops 1610612736 | bytes 8000000 | tf_op jit(solution)/shard_map/project/pallas_call | solution.py:354
  239.2 1.5 reshape.212
  240.7 4.2 %all-to-all-done.5.refs_2_ = bf16[16,256,128]{2,1,0:T(8,128)(2,1)S(1)} async-done(((bf16[16,256,128]{2,1,0:T(8,128)(2,1)}), bf16[16,256,128]{2,1,0:T(8,128)(2,1)S(1)}, u32[]{:S(2)}, u32[]{:S(2)}) %all-to-all-start.5) | async-done | bytes 1048608 | tf_op jit(solution)/shard_map/all_to_all | solution.py:420
  244.9 41.0 %all_to_all.42 = bf16[128,4,1024]{2,1,0:T(4,128)(2,1)} all-to-all(bf16[128,4,1024]{2,1,0:T(4,128)(2,1)S(1)} %reshape.212), channel_id=1, replica_groups=mesh['region'=16,'orbit'=8] {'region','orbit'}, dimensions={0} | all-to-all | bytes 2097152 | tf_op jit(solution)/shard_map/all_to_all | solution.py:420
  285.9 3.7 %all-to-all-start.4 = ((bf16[16,256,128]{2,1,0:T(8,128)(2,1)}), bf16[16,256,128]{2,1,0:T(8,128)(2,1)S(1)}, u32[]{:S(2)}, u32[]{:S(2)}) async-start(bf16[16,256,128]{2,1,0:T(8,128)(2,1)} %copy-done.4), calls=%async_computation.4 | async-start | bytes 2097152 | tf_op jit(solution)/shard_map/all_to_all | solution.py:420
  289.5 1.7 reduce_sum.42
  291.2 15.6 %all-to-all-done.4.refs_1_ = bf16[16,256,128]{2,1,0:T(8,128)(2,1)S(1)} async-done(((bf16[16,256,128]{2,1,0:T(8,128)(2,1)}), bf16[16,256,128]{2,1,0:T(8,128)(2,1)S(1)}, u32[]{:S(2)}, u32[]{:S(2)}) %all-to-all-start.4) | async-done | bytes 1048608 | tf_op jit(solution)/shard_map/all_to_all | solution.py:420
  308.1 5.8 %all-to-all-start.7 = ((bf16[128,4,1024]{2,1,0:T(4,128)(2,1)}), bf16[128,4,1024]{2,1,0:T(4,128)(2,1)}, u32[]{:S(2)}, u32[]{:S(2)}) async-start(bf16[128,4,1024]{2,1,0:T(4,128)(2,1)} %broadcast_in_dim.39), calls=%async_computation.7 | async-start | bytes 2097152 | tf_op jit(solution)/shard_map/all_to_all | solution.py:420
  313.9 2.0 unpack.1
  315.8 16.8 %all-to-all-done.7 = bf16[128,4,1024]{2,1,0:T(4,128)(2,1)} async-done(((bf16[128,4,1024]{2,1,0:T(4,128)(2,1)}), bf16[128,4,1024]{2,1,0:T(4,128)(2,1)}, u32[]{:S(2)}, u32[]{:S(2)}) %all-to-all-start.7) | async-done | bytes 1048608 | tf_op jit(solution)/shard_map/all_to_all | solution.py:420
  332.6 2.4 reshape.213
  (73 shorter events, 20.5 us)
Async XLA Ops:
  0.6 1.1 copy-start.7
  1.8 1.0 copy-start.12
  2.8 1.0 copy-start.13
  6.4 8.1 %copy-start.21 = (s32[1,3,8]{2,0,1:T(1,128)S(1)}, s32[1,3,8]{2,0,1:T(1,128)}, u32[]{:S(2)}) copy-start(s32[1,3,8]{2,0,1:T(1,128)} %param.10) | copy-start | bytes 292
  6.4 8.1 %copy-start.22 = (s32[1,3]{1,0:T(1,128)S(1)}, s32[1,3]{1,0:T(1,128)}, u32[]{:S(2)}) copy-start(s32[1,3]{1,0:T(1,128)} %param.11) | copy-start | bytes 40
  6.4 72.1 %all-to-all-start = ((bf16[16,704,128]{2,1,0:T(8,128)(2,1)}), bf16[16,704,128]{2,1,0:T(8,128)(2,1)S(1)}, u32[]{:S(2)}, u32[]{:S(2)}) async-start(bf16[16,704,128]{2,1,0:T(8,128)(2,1)} %pack.1), calls=%async_computation | async-start | bytes 5767168 | tf_op jit(solution)/shard_map/all_to_all | solution.py:420
  72.2 1.4 copy-start
  73.6 1.2 copy-start.2
  78.5 47.1 %all-to-all-start.2 = ((bf16[16,192,128]{2,1,0:T(8,128)(2,1)}), bf16[16,192,128]{2,1,0:T(8,128)(2,1)}, u32[]{:S(2)}, u32[]{:S(2)}) async-start(bf16[16,192,128]{2,1,0:T(8,128)(2,1)} %dattn.1), calls=%async_computation.2 | async-start | bytes 1572864 | tf_op jit(solution)/shard_map/all_to_all | solution.py:420
  122.4 1.3 copy-start.14
  125.6 1.1 copy-start.9
  126.7 1.6 copy-start.15
  128.3 1.2 copy-start.18
  129.5 1.1 copy-start.20
  130.7 32.6 %copy-start.10 = (bf16[48,64,128]{2,1,0:T(8,128)(2,1)S(1)}, bf16[48,64,128]{2,1,0:T(8,128)(2,1)}, u32[]{:S(2)}) copy-start(bf16[48,64,128]{2,1,0:T(8,128)(2,1)} %copy-done.8) | copy-start | bytes 2359300
  130.7 32.6 %copy-start.16 = (bf16[16,512,128]{2,1,0:T(8,128)(2,1)S(1)}, bf16[16,512,128]{2,1,0:T(8,128)(2,1)}, u32[]{:S(2)}) copy-start(bf16[16,512,128]{2,1,0:T(8,128)(2,1)} %copy-done.14) | copy-start | bytes 6291460
  195.1 33.3 %copy-start.5 = (bf16[16,256,128]{2,1,0:T(8,128)(2,1)}, bf16[16,256,128]{2,1,0:T(8,128)(2,1)S(1)}, u32[]{:S(2)}) copy-start(bf16[16,256,128]{2,1,0:T(8,128)(2,1)S(1)} %get-tuple-element.28) | copy-start | bytes 3145732
  213.4 18.6 %copy-start.3 = (bf16[512,1024]{1,0:T(8,128)(2,1)S(1)}, bf16[512,1024]{1,0:T(8,128)(2,1)}, u32[]{:S(2)}) copy-start(bf16[512,1024]{1,0:T(8,128)(2,1)} %w_ref.3) | copy-start | bytes 3145732
  228.4 16.5 %all-to-all-start.5 = ((bf16[16,256,128]{2,1,0:T(8,128)(2,1)}), bf16[16,256,128]{2,1,0:T(8,128)(2,1)S(1)}, u32[]{:S(2)}, u32[]{:S(2)}) async-start(bf16[16,256,128]{2,1,0:T(8,128)(2,1)} %copy-done.5), calls=%async_computation.5 | async-start | bytes 2097152 | tf_op jit(solution)/shard_map/all_to_all | solution.py:420
  232.0 1.4 copy-start.1
  233.4 1.1 copy-start.11
  238.2 1.0 copy-start.6
  285.9 21.0 %all-to-all-start.4 = ((bf16[16,256,128]{2,1,0:T(8,128)(2,1)}), bf16[16,256,128]{2,1,0:T(8,128)(2,1)S(1)}, u32[]{:S(2)}, u32[]{:S(2)}) async-start(bf16[16,256,128]{2,1,0:T(8,128)(2,1)} %copy-done.4), calls=%async_computation.4 | async-start | bytes 2097152 | tf_op jit(solution)/shard_map/all_to_all | solution.py:420
  308.1 24.5 %all-to-all-start.7 = ((bf16[128,4,1024]{2,1,0:T(4,128)(2,1)}), bf16[128,4,1024]{2,1,0:T(4,128)(2,1)}, u32[]{:S(2)}, u32[]{:S(2)}) async-start(bf16[128,4,1024]{2,1,0:T(4,128)(2,1)} %broadcast_in_dim.39), calls=%async_computation.7 | async-start | bytes 2097152 | tf_op jit(solution)/shard_map/all_to_all | solution.py:420
  (4 other events, 3.7 us)

commit v2 on v1

--- a/solution.py
+++ b/solution.py
@@ -1,5 +1,3 @@
-import functools
-
 import jax
 import jax.numpy as jnp
 from jax import lax
@@ -19,6 +17,13 @@
 D = 1024
 HW = 512
 CHUNKS = 2
+ROWS = BT // CHUNKS
+QUERY_ROWS = TILES_DEV * 64
+LIST_ROW = BT + QUERY_ROWS
+SEND_ROWS = LIST_ROW + 16
+DW_ROWS = HW * D // 16 // 128
+MID_ROWS = ROWS + DW_ROWS
+END_ROWS = QUERY_ROWS + ROWS + DW_ROWS
 PAIRS = 208
 SCALE = HEAD_DIM**-0.5
 LOW = -1e30
@@ -40,11 +45,14 @@
     return pl.CostEstimate(flops=int(flops), bytes_accessed=int(nbytes), transcendentals=int(exps))
 
 
-VMEM = pl.BlockSpec(memory_space=pltpu.VMEM)
+def whole(*shape):
+    return pl.BlockSpec(shape, lambda *_: (0,) * len(shape))
+
+
 SMEM = pl.BlockSpec(memory_space=pltpu.SMEM)
 
 
-def pack_body(q_ref, k_ref, v_ref, out_ref):
+def pack_body(q_ref, k_ref, v_ref, list_ref, out_ref):
     kt = k_ref[...].T
     vt = v_ref[...].T
     qt = (q_ref[...].astype(F32) * SCALE).astype(BF16).T
@@ -52,6 +60,7 @@
         rows = slice(head * 64, head * 64 + 64)
         for half in range(2):
             dest = 2 * head + half
+            out_ref[dest, LIST_ROW:SEND_ROWS, :] = list_ref[...]
             for j in range(4):
                 lanes = slice(j * 128, j * 128 + 128)
                 out_ref[dest, j * 128 : j * 128 + 64, :] = kt[rows, lanes]
@@ -61,8 +70,7 @@
                 out_ref[dest, BT + t * 64 : BT + t * 64 + 64, :] = qt[rows, low : low + HALF]
 
 
-def pack(q, k, v):
-    rows = BT + TILES_DEV * 64
+def pack(q, k, v, lists):
     return pl.pallas_call(
         pack_body,
         grid=(4,),
@@ -70,13 +78,14 @@
             pl.BlockSpec((TILES_DEV * QROWS, 128), lambda p: (0, p)),
             pl.BlockSpec((BT, 128), lambda p: (0, p)),
             pl.BlockSpec((BT, 128), lambda p: (0, p)),
-        ],
-        out_specs=pl.BlockSpec((4, rows, 128), lambda p: (p, 0, 0)),
-        out_shape=jax.ShapeDtypeStruct((16, rows, 128), BF16),
-        compiler_params=params(24),
+            pl.BlockSpec((16, 128), lambda p: (0, 0)),
+        ],
+        out_specs=pl.BlockSpec((4, SEND_ROWS, 128), lambda p: (p, 0, 0)),
+        out_shape=jax.ShapeDtypeStruct((16, SEND_ROWS, 128), BF16),
+        compiler_params=params(60),
         cost_estimate=cost(0, 8e6),
         name="pack",
-    )(q, k, v)
+    )(q, k, v, lists)
 
 
 def dattn_body(w_ref, g_ref, out_ref):
@@ -101,7 +110,7 @@
         ],
         out_specs=pl.BlockSpec((4, TILES_DEV * 64, 128), lambda p: (p, 0, 0)),
         out_shape=jax.ShapeDtypeStruct((16, TILES_DEV * 64, 128), BF16),
-        compiler_params=params(24),
+        compiler_params=params(60),
         cost_estimate=cost(2 * rows * D * HW, 4e6),
         name="dattn",
     )(w, g)
@@ -185,8 +194,15 @@
 def forward(plan, recv):
     return pl.pallas_call(
         forward_body,
-        in_specs=[SMEM, VMEM],
-        out_specs=[VMEM] * 5,
+        grid=(1,),
+        in_specs=[SMEM, whole(16, SEND_ROWS, 128)],
+        out_specs=[
+            whole(TILES, 64, HALF),
+            whole(TILES + 1, 1, HALF),
+            whole(BANDS, BT, 128),
+            whole(BANDS, 64, BT),
+            whole(TILES + 1, 64, HALF),
+        ],
         out_shape=[
             jax.ShapeDtypeStruct((TILES, 64, HALF), BF16),
             jax.ShapeDtypeStruct((TILES + 1, 1, HALF), F32),
@@ -202,13 +218,13 @@
             pltpu.VMEM((BT, 2 * HALF), F32),
             pltpu.VMEM((BT, 2 * HALF), F32),
         ],
-        compiler_params=params(40),
+        compiler_params=params(60),
         cost_estimate=cost(2.4e10, 2e7, 16e6),
         name="forward",
     )(plan, recv)
 
 
-def backward_body(last, plan, kv, kt, qt, dot_, attn, lse, dq_in, dkv_ref, dq_ref, w1, delta, dkv, dq, a0, c0, a1, c1):
+def backward_body(last, plan, kv, kt, qt, dot_, attn, lse, dq_in, send_ref, dq_ref, w1, delta, dkv, dq, a0, c0, a1, c1):
     rows = kv.shape[1]
 
     def prepare(x, carry):
@@ -261,71 +277,72 @@
 
     lax.fori_loop(0, plan[3, 0], two, 0)
 
+    first = QUERY_ROWS if last else 0
+
     def finish(b, carry):
-        dkv_ref[b] = dkv[b].astype(BF16)
+        send_ref[b, first : first + rows, :] = dkv[b].astype(BF16)
+        if last:
+            for t in range(TILES_DEV):
+                send_ref[b, t * 64 : t * 64 + 64, :] = (dq[b * TILES_DEV + t] * SCALE).astype(BF16)
         return carry
 
     lax.fori_loop(0, BANDS, finish, 0)
+    if not last:
+        dq_ref[...] = dq[...]
+
+
+def backward(chunk, plan, kv, kt, qt, dot_, attn, lse, dq_in=None):
+    last = chunk == CHUNKS - 1
     if last:
 
-        def finish_q(x, carry):
-            dq_ref[x] = (dq[x] * SCALE).astype(BF16)
-            return carry
-
-        lax.fori_loop(0, TILES, finish_q, 0)
+        def body(*refs):
+            return backward_body(True, *refs[:9], None, *refs[9:])
     else:
-        dq_ref[...] = dq[...]
-
-
-def backward(chunk, plan, kv, kt, qt, dot_, attn, lse, dq_in):
-    rows = BT // CHUNKS
-    last = chunk == CHUNKS - 1
-    first = dq_in is None
-    body = functools.partial(backward_body, last)
-    if first:
-        inner = body
-
-        def body(plan, kv, kt, qt, dot_, attn, lse, *rest):
-            return inner(plan, kv, kt, qt, dot_, attn, lse, None, *rest)
+
+        def body(*refs):
+            return backward_body(False, *refs[:7], None, *refs[7:])
 
     specs = [
         SMEM,
-        pl.BlockSpec((BANDS, rows, 128), lambda i: (0, chunk, 0)),
-        pl.BlockSpec((BANDS, 64, rows), lambda i: (0, 0, chunk)),
-        VMEM,
-        VMEM,
-        VMEM,
-        VMEM,
+        pl.BlockSpec((BANDS, ROWS, 128), lambda i: (0, chunk, 0)),
+        pl.BlockSpec((BANDS, 64, ROWS), lambda i: (0, 0, chunk)),
+        whole(TILES + 1, 64, HALF),
+        whole(TILES, 64, HALF),
+        whole(TILES, 64, HALF),
+        whole(TILES + 1, 1, HALF),
     ]
     args = [plan, kv, kt, qt, dot_, attn, lse]
-    if not first:
-        specs.append(VMEM)
+    if last:
+        specs.append(whole(TILES + 1, 64, HALF))
         args.append(dq_in)
-    dq_shape = (
-        jax.ShapeDtypeStruct((TILES, 64, HALF), BF16)
-        if last
-        else jax.ShapeDtypeStruct((TILES + 1, 64, HALF), F32)
-    )
+        out_specs = [whole(BANDS, QUERY_ROWS + ROWS, 128)]
+        out_shape = [jax.ShapeDtypeStruct((BANDS, END_ROWS, 128), BF16)]
+    else:
+        out_specs = [whole(BANDS, ROWS, 128), whole(TILES + 1, 64, HALF)]
+        out_shape = [
+            jax.ShapeDtypeStruct((BANDS, MID_ROWS, 128), BF16),
+            jax.ShapeDtypeStruct((TILES + 1, 64, HALF), F32),
+        ]
     return pl.pallas_call(
         body,
         grid=(1,),
         in_specs=specs,
-        out_specs=[VMEM, VMEM],
-        out_shape=[jax.ShapeDtypeStruct((BANDS, rows, 128), BF16), dq_shape],
+        out_specs=out_specs,
+        out_shape=out_shape,
         scratch_shapes=[
             pltpu.VMEM((TILES + 1, 128, 2 * HALF), BF16),
             pltpu.VMEM((TILES + 1, 1, HALF), F32),
-            pltpu.VMEM((BANDS, rows, 128), F32),
+            pltpu.VMEM((BANDS, ROWS, 128), F32),
             pltpu.VMEM((TILES + 1, 64, HALF), F32),
         ]
-        + [pltpu.VMEM((rows, 2 * HALF), F32)] * 4,
-        compiler_params=params(40),
+        + [pltpu.VMEM((ROWS, 2 * HALF), F32)] * 4,
+        compiler_params=params(60),
         cost_estimate=cost(5e10 / CHUNKS, 2e7, 16e6 / CHUNKS),
         name="backward",
     )(*args)
 
 
-def project_body(recv, w_ref, g_ref, layer_ref, dw_ref, acc):
+def project_body(recv, w_ref, g_ref, unused, layer_ref, send_ref, acc):
     t = pl.program_id(0)
     low = pl.multiple_of(t * 64, 64)
     heads = [
@@ -346,10 +363,15 @@
 
     @pl.when(t == TILES_DEV - 1)
     def _():
-        dw_ref[...] = acc[...].astype(BF16)
-
-
-def project(recv, w, g):
+        wide = D // 128
+        for dest in range(16):
+            for j in range(wide):
+                send_ref[dest, j * 32 : j * 32 + 32, :] = acc[
+                    dest * 32 : dest * 32 + 32, j * 128 : j * 128 + 128
+                ].astype(BF16)
+
+
+def project(recv, w, g, send):
     rows = TILES_DEV * QROWS
     return pl.pallas_call(
         project_body,
@@ -358,91 +380,127 @@
             pl.BlockSpec((16, TILES_DEV * 64, 128), lambda t: (0, 0, 0)),
             pl.BlockSpec((HW, D), lambda t: (0, 0)),
             pl.BlockSpec((QROWS, D), lambda t: (t, 0)),
+            pl.BlockSpec(memory_space=pl.ANY),
         ],
         out_specs=[
             pl.BlockSpec((QROWS, D), lambda t: (t, 0)),
-            pl.BlockSpec((HW, D), lambda t: (0, 0)),
-        ],
-        out_shape=[jax.ShapeDtypeStruct((rows, D), BF16), jax.ShapeDtypeStruct((HW, D), BF16)],
+            pl.BlockSpec((16, DW_ROWS, 128), lambda t: (0, ROWS // DW_ROWS, 0)),
+        ],
+        out_shape=[
+            jax.ShapeDtypeStruct((rows, D), BF16),
+            jax.ShapeDtypeStruct((BANDS, MID_ROWS, 128), BF16),
+        ],
+        input_output_aliases={3: 1},
         scratch_shapes=[pltpu.VMEM((HW, D), F32)],
-        compiler_params=params(40),
+        compiler_params=params(60),
         cost_estimate=cost(4 * rows * D * HW, 8e6),
         name="project",
-    )(recv, w, g)
-
-
-def unpack_body(*refs):
-    dq_in, parts = refs[0], refs[1 : 1 + CHUNKS]
-    dq_ref, dk_ref, dv_ref = refs[1 + CHUNKS :]
+    )(recv, w, g, send)
+
+
+def spread_body(part_ref, unused, send_ref):
+    total = jnp.sum(part_ref[...].astype(F32), axis=0).astype(BF16)
+    for dest in range(16):
+        send_ref[dest] = total
+
+
+def spread(part, send):
+    return pl.pallas_call(
+        spread_body,
+        grid=(DW_ROWS // 64,),
+        in_specs=[
+            pl.BlockSpec((part.shape[0], 64, 128), lambda i: (0, i, 0)),
+            pl.BlockSpec(memory_space=pl.ANY),
+        ],
+        out_specs=pl.BlockSpec((16, 64, 128), lambda i: (0, (END_ROWS - DW_ROWS) // 64 + i, 0)),
+        out_shape=jax.ShapeDtypeStruct((BANDS, END_ROWS, 128), BF16),
+        input_output_aliases={1: 0},
+        compiler_params=params(60),
+        cost_estimate=cost(0, 2e6),
+        name="spread",
+    )(part, send)
+
+
+def unpack_body(mid, end, dq_ref, dk_ref, dv_ref, dw_ref):
     heads = []
     for head in range(2):
         blocks = []
         for t in range(TILES_DEV):
             for half in range(2):
-                blocks.append(dq_in[2 * head + half, t * 64 : t * 64 + 64, :])
+                blocks.append(end[2 * head + half, t * 64 : t * 64 + 64, :])
         heads.append(jnp.concatenate(blocks, axis=1))
     dq_ref[...] = jnp.concatenate(heads, axis=0).T
-    rows = BT // CHUNKS
-    left = lax.broadcasted_iota(jnp.int32, (rows, 128), 1) < 64
-    for chunk in range(CHUNKS):
-        part = parts[chunk]
-        x = part[0].astype(F32) + part[1].astype(F32)
-        y = part[2].astype(F32) + part[3].astype(F32)
-        at = slice(chunk * rows, chunk * rows + rows)
+    left = lax.broadcasted_iota(jnp.int32, (ROWS, 128), 1) < 64
+    for chunk, part, low in ((0, mid, 0), (1, end, QUERY_ROWS)):
+        take = [part[r, low : low + ROWS, :].astype(F32) for r in range(4)]
+        x, y = take[0] + take[1], take[2] + take[3]
+        at = slice(chunk * ROWS, chunk * ROWS + ROWS)
         dk_ref[at, :] = jnp.where(left, x, pltpu.roll(y, 64, 1)).astype(BF16)
         dv_ref[at, :] = jnp.where(left, pltpu.roll(x, 64, 1), y).astype(BF16)
-
-
-def unpack(dq, parts):
+    for r in range(4):
+        for j in range(D // 128):
+            at = END_ROWS - DW_ROWS + j * 32
+            dw_ref[r * 32 : r * 32 + 32, j * 128 : j * 128 + 128] = end[r, at : at + 32, :].astype(F32)
+
+
+def unpack(mid, end):
     rows = TILES_DEV * QROWS
     return pl.pallas_call(
         unpack_body,
         grid=(4,),
-        in_specs=[pl.BlockSpec((4, TILES_DEV * 64, 128), lambda p: (p, 0, 0))]
-        + [pl.BlockSpec((4, BT // CHUNKS, 128), lambda p: (p, 0, 0))] * CHUNKS,
+        in_specs=[
+            pl.BlockSpec((4, ROWS, 128), lambda p: (p, 0, 0)),
+            pl.BlockSpec((4, END_ROWS, 128), lambda p: (p, 0, 0)),
+        ],
         out_specs=[
             pl.BlockSpec((rows, 128), lambda p: (0, p)),
             pl.BlockSpec((BT, 128), lambda p: (0, p)),
             pl.BlockSpec((BT, 128), lambda p: (0, p)),
+            pl.BlockSpec((128, D), lambda p: (p, 0)),
         ],
         out_shape=[
             jax.ShapeDtypeStruct((rows, HW), BF16),
             jax.ShapeDtypeStruct((BT, HW), BF16),
             jax.ShapeDtypeStruct((BT, HW), BF16),
-        ],
-        compiler_params=params(24),
+            jax.ShapeDtypeStruct((HW, D), F32),
+        ],
+        compiler_params=params(60),
         cost_estimate=cost(0, 8e6),
         name="unpack",
-    )(dq, *parts)
+    )(mid, end)
 
 
 def swap(x, axes="region"):
     return lax.all_to_all(x, axes, 0, 0, tiled=True)
 
 
-def per_device(devices, queries, keys, values, block_lists, band_counts, cotangent, out_weight):
+def per_device(queries, keys, values, block_lists, band_counts, cotangent, out_weight):
     rows = TILES_DEV * QROWS
     q, g = queries.reshape(rows, HW), cotangent.reshape(rows, D)
-    recv1 = swap(pack(q, keys.reshape(BT, HW), values.reshape(BT, HW)))
-    recv2 = swap(dattn(out_weight, g)).reshape(TILES, 64, HALF)
-    where = jnp.concatenate([block_lists[0], band_counts[0][:, None]], axis=1)
-    where = lax.all_gather(where, "region", axis=0, tiled=True)
-    plan = plan_of(where[:, :MAXB], where[:, MAXB])
-
-    attn, lse, kv, kt, qt = forward(plan, recv1)
-    recv3 = swap(attn.reshape(16, TILES_DEV * 64, HALF))
-    dq = None
-    parts = []
-    for chunk in range(CHUNKS):
-        part, dq = backward(chunk, plan, kv, kt, qt, recv2, attn, lse, dq)
-        parts.append(swap(part))
-    layer, dw = project(recv3, out_weight, g)
-    dw = swap(dw.reshape(devices, HW // devices, D), ("region", "orbit"))
-    dw = jnp.sum(dw.astype(F32), axis=0, keepdims=True).astype(BF16)
-    dw = swap(jnp.broadcast_to(dw, (devices, HW // devices, D)), ("region", "orbit"))
-    d_weight = dw.reshape(HW, D).astype(F32)
-    dq = swap(dq.reshape(16, TILES_DEV * 64, HALF))
-    d_q, d_k, d_v = unpack(dq, parts)
+    lists = jnp.concatenate([block_lists[0], band_counts[0][:, None]], axis=1).astype(BF16)
+    lists = lists.reshape(1, -1)
+    lists = jnp.pad(lists, ((0, 15), (0, 128 - lists.shape[1])))
+    recv = swap(pack(q, keys.reshape(BT, HW), values.reshape(BT, HW), lists))
+    lists = recv[:, LIST_ROW, : TILES_DEV * (MAXB + 1)].astype(jnp.int32).reshape(TILES, MAXB + 1)
+    plan = plan_of(lists[:, :MAXB], lists[:, MAXB])
+    d_attn = dattn(out_weight, g)
+    recv, d_attn = lax.optimization_barrier((recv, d_attn))
+    d_attn = swap(d_attn).reshape(TILES, 64, HALF)
+
+    attn, lse, kv, kt, qt = forward(plan, recv)
+    attn_home = swap(attn.reshape(16, QUERY_ROWS, HALF))
+    mid, dq = backward(0, plan, kv, kt, qt, d_attn, attn, lse)
+    attn_home, mid = lax.optimization_barrier((attn_home, mid))
+    layer, mid = project(attn_home, out_weight, g, mid)
+    mid, dq = lax.optimization_barrier((mid, dq))
+    mid = swap(mid)
+    (end,) = backward(1, plan, kv, kt, qt, d_attn, attn, lse, dq)
+    mid, end = lax.optimization_barrier((mid, end))
+    share = jnp.sum(mid[:, ROWS:].astype(F32), axis=0, keepdims=True).astype(BF16)
+    orbits = lax.axis_size("orbit")
+    share = swap(jnp.broadcast_to(share, (orbits, DW_ROWS, 128)), "orbit")
+    end = swap(spread(share, end))
+    d_q, d_k, d_v, d_weight = unpack(mid, end)
     return (
         layer.reshape(1, TILES_DEV, QROWS, D),
         d_q.reshape(1, TILES_DEV, QROWS, HW),
@@ -455,7 +513,7 @@
 def solution(mesh):
     four = P("orbit", "region", None, None)
     return jax.shard_map(
-        functools.partial(per_device, mesh.devices.size),
+        per_device,
         mesh=mesh,
         in_specs=(four, four, four, P("orbit", "region", None), P("orbit", "region"), four, P()),
         out_specs=(four, four, four, four, P()),

time: 334 us -> 269 us (0.81)
  blocking collectives: 129 us -> 62.8 us
  local copies, waits for them, and re-layouts: 25.5 us -> 2.56 us
  Pallas kernels: 112 us -> 134 us
    all_gather x1 -> x0, blocking collectives: 54.7 us -> none  [per_device(): where = lax.all_gather(where, 'region', axis=0, tiled=True)]
    unnamed x48 -> x7, local copies, waits for them, and re-layouts: 19.5 us -> 0.89 us
    pallas_call x4 -> x5, Pallas kernels: 103 us -> 119 us  [the longest x2 69.3 us: backward(): pl.pallas_call(body, grid=(1,), in_specs=specs, out_specs=out_specs, out_...]
    all_to_all x3 -> x2, blocking collectives: 74.2 us -> 62.8 us  [swap(): return lax.all_to_all(x, axes, 0, 0, tiled=True)]
    all_to_all x5 -> x4, starting transfers between devices: 26.9 us -> 29 us  [swap(): return lax.all_to_all(x, axes, 0, 0, tiled=True)]
    all_to_all x5 -> x4, waiting for transfers between devices: 36.6 us -> 35.2 us  [swap(): return lax.all_to_all(x, axes, 0, 0, tiled=True)]
  transfers between devices with their start and end apart: 5 -> 4, of which waited for: 3 -> 1; matrix products, arithmetic and copies ran while one was open for 2% -> 0% of each run, Pallas kernels for 14% -> 43%
where the time goes in v2:
time: 269 us
  Pallas kernels  134 us (50%)
  blocking collectives  62.8 us (23%)
  waiting for transfers between devices  35.2 us (13%)
  starting transfers between devices  29 us (11%)
  other arithmetic  4.23 us (2%)
    pallas_call x2, Pallas kernels, backward(): pl.pallas_call(body, grid=(1,), in_specs=specs, out_specs=out_specs, out_...  69.3 us
    all_to_all x2, blocking collectives, swap(): return lax.all_to_all(x, axes, 0, 0, tiled=True)  62.8 us
    pallas_call x1, Pallas kernels, forward(): pl.pallas_call(forward_body, grid=(1,), in_specs=[SMEM, whole(16, SEND_RO...  41.2 us
    all_to_all x4, waiting for transfers between devices, swap(): return lax.all_to_all(x, axes, 0, 0, tiled=True)  35.2 us
    all_to_all x4, starting transfers between devices, swap(): return lax.all_to_all(x, axes, 0, 0, tiled=True)  29 us
    pallas_call x1, Pallas kernels, project(): pl.pallas_call(project_body, grid=(TILES_DEV,), in_specs=[pl.BlockSpec((1...  5.9 us
  transfers between devices with their start and end apart: 4, of which 1 were waited for; matrix products, arithmetic and copies ran while one was open for 0% of the time, Pallas kernels for 43%

profile of v2, /device:TPU:0, one launch (start us, length us, event | category | flops | bytes accessed | tf_op | source)
XLA Modules:
  0.0 269.1 jit_solution(6675468961087094965)
XLA Ops:
  0.6 0.7 convert_bitcast_fusion.1
  1.4 0.7 convert.10
  2.3 0.6 pad.4.list_ref
  2.9 4.3 %pack.1 = bf16[16,720,128]{2,1,0:T(8,128)(2,1)} custom-call(bf16[768,512]{1,0:T(8,128)(2,1)} %bitcast.35, bf16[512,512]{1,0:T(8,128)(2,1)} %bitcast.36, bf16[512,512]{1,0:T(8,128)(2,1)} %bitcast.37, bf16[16,128]{1,0:T(8,128)(2,1)} %pad.4.list_ref), custom_call_target="tpu_custom_call" | custom-call | bytes 8000000 | tf_op jit(solution)/shard_map/pack/pallas_call | solution.py:74
  7.1 8.0 %all-to-all-start = ((bf16[16,720,128]{2,1,0:T(8,128)(2,1)}), bf16[16,720,128]{2,1,0:T(8,128)(2,1)S(1)}, u32[]{:S(2)}, u32[]{:S(2)}) async-start(bf16[16,720,128]{2,1,0:T(8,128)(2,1)} %pack.1), calls=%async_computation | async-start | bytes 5898240 | tf_op jit(solution)/shard_map/all_to_all | solution.py:474
  15.1 5.2 %dattn.1 = bf16[16,192,128]{2,1,0:T(8,128)(2,1)} custom-call(bf16[512,1024]{1,0:T(8,128)(2,1)} %w_ref.3, bf16[768,1024]{1,0:T(8,128)(2,1)} %bitcast.32), custom_call_target="tpu_custom_call" | custom-call | flops 805306368 | bytes 4000000 | tf_op jit(solution)/shard_map/dattn/pallas_call | solution.py:104
  20.3 35.2 %all-to-all-done.recv = bf16[16,720,128]{2,1,0:T(8,128)(2,1)S(1)} async-done(((bf16[16,720,128]{2,1,0:T(8,128)(2,1)}), bf16[16,720,128]{2,1,0:T(8,128)(2,1)S(1)}, u32[]{:S(2)}, u32[]{:S(2)}) %all-to-all-start) | async-done | bytes 2949152 | tf_op jit(solution)/shard_map/all_to_all | solution.py:474
  56.0 1.0 fusion.4
  57.9 0.2 reduce_window_sum.18
  58.1 0.3 select_reduce_fusion
  58.7 6.7 %all-to-all-start.2 = ((bf16[16,192,128]{2,1,0:T(8,128)(2,1)}), bf16[16,192,128]{2,1,0:T(8,128)(2,1)}, u32[]{:S(2)}, u32[]{:S(2)}) async-start(bf16[16,192,128]{2,1,0:T(8,128)(2,1)} %dattn.1), calls=%async_computation.2 | async-start | bytes 1572864 | tf_op jit(solution)/shard_map/all_to_all | solution.py:474
  65.5 0.2 slice_reduce_fusion.2
  65.7 0.7 add_add_fusion.1.plan.refs_0_
  66.4 41.2 %forward.1 = (bf16[48,64,128]{2,1,0:T(8,128)(2,1)}, f32[49,1,128]{2,1,0:T(1,128)}, bf16[16,512,128]{2,1,0:T(8,128)(2,1)}, bf16[16,64,512]{2,1,0:T(8,128)(2,1)}, bf16[49,64,128]{2,1,0:T(8,128)(2,1)}) custom-call(s32[4,208]{1,0:T(4,128)} %add_add_fusion.1.plan.refs_0_, bf16[16,720,128]{2,1,0:T(8,128)(2,1)} %copy-done.1), custom_call_target="tpu_custom_call" | custom-call | flops 24000000000 | bytes 20000000 | tf_op jit(solution)/shard_map/forward/pallas_call | solution.py:195
  107.6 7.2 %all-to-all-start.1 = ((bf16[16,192,128]{2,1,0:T(8,128)(2,1)}), bf16[16,192,128]{2,1,0:T(8,128)(2,1)S(1)}, u32[]{:S(2)}, u32[]{:S(2)}) async-start(bf16[16,192,128]{2,1,0:T(8,128)(2,1)} %bitcast.34), calls=%async_computation.1 | async-start | bytes 1572864 | tf_op jit(solution)/shard_map/all_to_all | solution.py:474
  114.8 34.5 %backward.2 = (bf16[16,512,128]{2,1,0:T(8,128)(2,1)}, f32[49,64,128]{2,1,0:T(8,128)}) custom-call(s32[4,208]{1,0:T(4,128)} %add_add_fusion.1.plan.refs_0_, bf16[16,512,128]{2,1,0:T(8,128)(2,1)} %get-tuple-element.28.refs_1_, bf16[16,64,512]{2,1,0:T(8,128)(2,1)} %get-tuple-element.29.refs_2_, bf16[49,64,128]{2,1,0:T(8,128)(2,1)} %get-tuple-element.30.refs_3_, ...), custom_call_target="tpu_custom_call" | custom-call | flops 24999999488 | bytes 20000000 | tf_op jit(solution)/shard_map/backward/pallas_call | solution.py:326
  149.2 0.9 copy-done.2
  150.1 5.9 %project.1 = (bf16[768,1024]{1,0:T(8,128)(2,1)}, bf16[16,512,128]{2,1,0:T(8,128)(2,1)}) custom-call(bf16[16,192,128]{2,1,0:T(8,128)(2,1)} %copy-done.2, bf16[512,1024]{1,0:T(8,128)(2,1)} %w_ref.3, bf16[768,1024]{1,0:T(8,128)(2,1)} %bitcast.33, bf16[16,512,128]{2,1,0:T(8,128)(2,1)} %get-tuple-element.35.unused), custom_call_target="tpu_custom_call", output_to_operand_aliasing={{1}: (3, {})} | custom-call | flops 1610612736 | bytes 8000000 | tf_op jit(solution)/shard_map/project/pallas_call | solution.py:376
  156.0 7.2 %all-to-all-start.3 = ((bf16[16,512,128]{2,1,0:T(8,128)(2,1)}), bf16[16,512,128]{2,1,0:T(8,128)(2,1)S(1)}, u32[]{:S(2)}, u32[]{:S(2)}) async-start(bf16[16,512,128]{2,1,0:T(8,128)(2,1)} %get-tuple-element.39), calls=%async_computation.3 | async-start | bytes 4194304 | tf_op jit(solution)/shard_map/all_to_all | solution.py:474
  163.2 34.9 %backward.3.unused = bf16[16,704,128]{2,1,0:T(8,128)(2,1)} custom-call(s32[4,208]{1,0:T(4,128)} %add_add_fusion.1.plan.refs_0_, bf16[16,512,128]{2,1,0:T(8,128)(2,1)} %get-tuple-element.28.refs_1_, bf16[16,64,512]{2,1,0:T(8,128)(2,1)} %get-tuple-element.29.refs_2_, bf16[49,64,128]{2,1,0:T(8,128)(2,1)} %get-tuple-element.30.refs_3_, ...), custom_call_target="tpu_custom_call" | custom-call | flops 24999999488 | bytes 20000000 | tf_op jit(solution)/shard_map/backward/pallas_call | solution.py:326
  198.3 19.3 %all_to_all.30.part_ref = bf16[8,256,128]{2,1,0:T(8,128)(2,1)} all-to-all(bf16[8,256,128]{2,1,0:T(8,128)(2,1)S(1)} %broadcast_in_dim.39), channel_id=1, replica_groups=mesh['region'=16,'orbit'=8] {'orbit'}, dimensions={0} | all-to-all | bytes 1048576 | tf_op jit(solution)/shard_map/all_to_all | solution.py:474
  217.6 3.3 %spread.1 = bf16[16,704,128]{2,1,0:T(8,128)(2,1)} custom-call(bf16[8,256,128]{2,1,0:T(8,128)(2,1)} %all_to_all.30.part_ref, bf16[16,704,128]{2,1,0:T(8,128)(2,1)} %backward.3.unused), custom_call_target="tpu_custom_call", output_to_operand_aliasing={{}: (1, {})} | custom-call | bytes 2000000 | tf_op jit(solution)/shard_map/spread/pallas_call | solution.py:408
  221.0 43.5 %all_to_all.31.end = bf16[16,704,128]{2,1,0:T(8,128)(2,1)} all-to-all(bf16[16,704,128]{2,1,0:T(8,128)(2,1)} %spread.1), channel_id=1, replica_groups=mesh['region'=16,'orbit'=8] {'region'}, dimensions={0} | all-to-all | bytes 5767168 | tf_op jit(solution)/shard_map/all_to_all | solution.py:474
  264.5 4.6 %unpack.1 = (bf16[768,512]{1,0:T(8,128)(2,1)}, bf16[512,512]{1,0:T(8,128)(2,1)}, bf16[512,512]{1,0:T(8,128)(2,1)}, f32[512,1024]{1,0:T(8,128)}) custom-call(bf16[16,512,128]{2,1,0:T(8,128)(2,1)} %copy-done, bf16[16,704,128]{2,1,0:T(8,128)(2,1)} %all_to_all.31.end), custom_call_target="tpu_custom_call" | custom-call | bytes 8000000 | tf_op jit(solution)/shard_map/unpack/pallas_call | solution.py:448
  (33 shorter events, 1.7 us)
Async XLA Ops:
  7.1 48.3 %all-to-all-start = ((bf16[16,720,128]{2,1,0:T(8,128)(2,1)}), bf16[16,720,128]{2,1,0:T(8,128)(2,1)S(1)}, u32[]{:S(2)}, u32[]{:S(2)}) async-start(bf16[16,720,128]{2,1,0:T(8,128)(2,1)} %pack.1), calls=%async_computation | async-start | bytes 5898240 | tf_op jit(solution)/shard_map/all_to_all | solution.py:474
  55.5 10.9 %copy-start.1 = (bf16[16,720,128]{2,1,0:T(8,128)(2,1)}, bf16[16,720,128]{2,1,0:T(8,128)(2,1)S(1)}, u32[]{:S(2)}) copy-start(bf16[16,720,128]{2,1,0:T(8,128)(2,1)S(1)} %all-to-all-done.recv) | copy-start | bytes 8847364
  58.7 48.9 %all-to-all-start.2 = ((bf16[16,192,128]{2,1,0:T(8,128)(2,1)}), bf16[16,192,128]{2,1,0:T(8,128)(2,1)}, u32[]{:S(2)}, u32[]{:S(2)}) async-start(bf16[16,192,128]{2,1,0:T(8,128)(2,1)} %dattn.1), calls=%async_computation.2 | async-start | bytes 1572864 | tf_op jit(solution)/shard_map/all_to_all | solution.py:474
  107.6 41.6 %all-to-all-start.1 = ((bf16[16,192,128]{2,1,0:T(8,128)(2,1)}), bf16[16,192,128]{2,1,0:T(8,128)(2,1)S(1)}, u32[]{:S(2)}, u32[]{:S(2)}) async-start(bf16[16,192,128]{2,1,0:T(8,128)(2,1)} %bitcast.34), calls=%async_computation.1 | async-start | bytes 1572864 | tf_op jit(solution)/shard_map/all_to_all | solution.py:474
  149.2 0.9 copy-start.2
  156.0 42.1 %all-to-all-start.3 = ((bf16[16,512,128]{2,1,0:T(8,128)(2,1)}), bf16[16,512,128]{2,1,0:T(8,128)(2,1)S(1)}, u32[]{:S(2)}, u32[]{:S(2)}) async-start(bf16[16,512,128]{2,1,0:T(8,128)(2,1)} %get-tuple-element.39), calls=%async_computation.3 | async-start | bytes 4194304 | tf_op jit(solution)/shard_map/all_to_all | solution.py:474
  198.1 22.9 %copy-start = (bf16[16,512,128]{2,1,0:T(8,128)(2,1)}, bf16[16,512,128]{2,1,0:T(8,128)(2,1)S(1)}, u32[]{:S(2)}) copy-start(bf16[16,512,128]{2,1,0:T(8,128)(2,1)S(1)} %all-to-all-done.3.mid) | copy-start | bytes 6291460

commit v3 on v2

--- a/solution.py
+++ b/solution.py
@@ -1,3 +1,5 @@
+import functools
+
 import jax
 import jax.numpy as jnp
 from jax import lax
@@ -17,6 +19,11 @@
 D = 1024
 HW = 512
 CHUNKS = 2
+UNROLL = 8
+BACK_UNROLL = 8
+SUB = 64
+BACK_SUB = 256
+SUM_ROWS = 16
 ROWS = BT // CHUNKS
 QUERY_ROWS = TILES_DEV * 64
 LIST_ROW = BT + QUERY_ROWS
@@ -131,18 +138,18 @@
     band = jnp.arange(BANDS)[None, :, None]
     code = jnp.sum(jnp.where(hit, band * 64 + tile + 1, 0), axis=(1, 2)).reshape(PAIRS, 2)
     who = jnp.where(code > 0, (code & 63) - 1, TILES)
-    number = (size.sum() + 1) // 2
+    number = size.sum()
     return jnp.stack(
         [who[:, 0], who[:, 1], code[:, 0] >> 6, jnp.full((PAIRS,), number, jnp.int32)]
     ).astype(jnp.int32)
 
 
-def forward_body(plan, recv, attn_ref, lse_ref, kv_ref, kt_ref, qt_ref, vt, top, total, acc, s0, s1):
+def forward_body(plan, recv, attn_ref, lse_ref, kv_ref, kt_ref, qt_ref, vt, top, acc, s0, s1, p0, p1, h0, h1):
     def unpack_band(b, carry):
         kvt = jnp.concatenate([recv[b, j * 128 : j * 128 + 128, :] for j in range(4)], axis=1)
         kv_ref[b] = kvt.T
         kt_ref[b] = kvt[:64]
-        vt[b] = kvt[64:]
+        vt[b] = jnp.concatenate([kvt[64:], jnp.ones((SUM_ROWS, BT), BF16)], axis=0)
         for t in range(TILES_DEV):
             qt_ref[b * TILES_DEV + t] = recv[b, BT + t * 64 : BT + t * 64 + 64, :]
         return carry
@@ -150,41 +157,57 @@
     lax.fori_loop(0, BANDS, unpack_band, 0)
     qt_ref[TILES] = jnp.zeros((64, HALF), BF16)
     top[...] = jnp.full(top.shape, LOW, F32)
-    total[...] = jnp.zeros(total.shape, F32)
     acc[...] = jnp.zeros(acc.shape, F32)
     blank = jnp.zeros((64, 2 * HALF), BF16)
 
-    def scores(i, dst):
-        w = jnp.concatenate([qt_ref[plan[0, i]], qt_ref[plan[1, i]]], axis=1)
-        dst[...] = dot(kv_ref[plan[2, i]], jnp.concatenate([w, blank], axis=0))
-
-    def absorb(i, src):
-        a, c, b = plan[0, i], plan[1, i], plan[2, i]
+    def scores(i, s, h, weigh=None):
+        a, c = plan[0, i], plan[1, i]
+        w = jnp.concatenate([jnp.concatenate([qt_ref[a], qt_ref[c]], axis=1), blank], axis=0)
+        peak = None
+        for low in range(0, BT, SUB):
+            rows = slice(low, low + SUB)
+            st = dot(kv_ref[plan[2, i], rows, :], w)
+            s[rows, :] = st
+            high = jnp.max(st.reshape(SUB // 8, 8, 2 * HALF), axis=0)
+            peak = high if peak is None else jnp.maximum(peak, high)
+            if weigh is not None:
+                weigh(rows)
         old = jnp.concatenate([top[a], top[c]], axis=1)
-        new = jnp.maximum(old, jnp.max(src[...], axis=0, keepdims=True))
-        fade = jnp.exp(old - new)
-        p = jnp.exp(src[...] - new)
-        part = jnp.sum(p, axis=0, keepdims=True)
-        o = dot(vt[b], p.astype(BF16))
-        for x, lanes in ((a, slice(0, HALF)), (c, slice(HALF, 2 * HALF))):
-            top[x] = new[:, lanes]
-            total[x] = total[x] * fade[:, lanes] + part[:, lanes]
+        new = jnp.maximum(old, jnp.max(peak, axis=0, keepdims=True))
+        top[a] = new[:, :HALF]
+        top[c] = new[:, HALF:]
+        h[0:1, :] = new
+        h[1:2, :] = jnp.exp(old - new)
+
+    def weigh(s, h, p, rows):
+        p[rows, :] = jnp.exp(s[rows, :] - h[0:1, :]).astype(BF16)
+
+    def gather(i, fade, p):
+        o = dot(vt[plan[2, i]], p[...])
+        for x, lanes in ((plan[0, i], slice(0, HALF)), (plan[1, i], slice(HALF, 2 * HALF))):
             acc[x] = acc[x] * fade[:, lanes] + o[:, lanes]
 
-    scores(0, s0)
-
-    def two(j, carry):
-        scores(2 * j + 1, s1)
-        absorb(2 * j, s0)
-        scores(2 * j + 2, s0)
-        absorb(2 * j + 1, s1)
+    scores(0, s0, h0)
+    scores(1, s1, h1)
+    weigh(s0, h0, p0, slice(0, BT))
+
+    even, odd = (s0, h0, p0), (s1, h1, p1)
+
+    def step(j, carry):
+        for k in range(UNROLL):
+            i = UNROLL * j + k
+            (s, h, p), (s_next, h_next, p_next) = (even, odd) if k % 2 == 0 else (odd, even)
+            fade = h[1:2, :]
+            scores(i + 2, s, h, functools.partial(weigh, s_next, h_next, p_next))
+            gather(i, fade, p)
         return carry
 
-    lax.fori_loop(0, plan[3, 0], two, 0)
+    lax.fori_loop(0, (plan[3, 0] + UNROLL - 1) // UNROLL, step, 0)
 
     def finish(x, carry):
-        attn_ref[x] = (acc[x] / total[x]).astype(BF16)
-        lse_ref[x] = top[x] + jnp.log(total[x])
+        total = acc[x, 64:65, :]
+        attn_ref[x] = (acc[x, :64, :] / total).astype(BF16)
+        lse_ref[x] = top[x] + jnp.log(total)
         return carry
 
     lax.fori_loop(0, TILES, finish, 0)
@@ -211,12 +234,15 @@
             jax.ShapeDtypeStruct((TILES + 1, 64, HALF), BF16),
         ],
         scratch_shapes=[
-            pltpu.VMEM((BANDS, 64, BT), BF16),
+            pltpu.VMEM((BANDS, 64 + SUM_ROWS, BT), BF16),
             pltpu.VMEM((TILES + 1, 1, HALF), F32),
-            pltpu.VMEM((TILES + 1, 1, HALF), F32),
-            pltpu.VMEM((TILES + 1, 64, HALF), F32),
+            pltpu.VMEM((TILES + 1, 64 + SUM_ROWS, HALF), F32),
             pltpu.VMEM((BT, 2 * HALF), F32),
             pltpu.VMEM((BT, 2 * HALF), F32),
+            pltpu.VMEM((BT, 2 * HALF), BF16),
+            pltpu.VMEM((BT, 2 * HALF), BF16),
+            pltpu.VMEM((8, 2 * HALF), F32),
+            pltpu.VMEM((8, 2 * HALF), F32),
         ],
         compiler_params=params(60),
         cost_estimate=cost(2.4e10, 2e7, 16e6),
@@ -224,63 +250,73 @@
     )(plan, recv)
 
 
-def backward_body(last, plan, kv, kt, qt, dot_, attn, lse, dq_in, send_ref, dq_ref, w1, delta, dkv, dq, a0, c0, a1, c1):
+def backward_body(last, plan, kv, kt, qt, dot_, attn, lse, dq_in, send_ref, dq_ref, gt, delta, dkv, dq, s0, t0, s1, t1, p0, d0, p1, d1):
     rows = kv.shape[1]
 
     def prepare(x, carry):
-        blank = jnp.zeros((64, HALF), BF16)
-        w1[x] = jnp.concatenate(
-            [jnp.concatenate([qt[x], blank], axis=1), jnp.concatenate([blank, dot_[x]], axis=1)], axis=0
-        )
+        gt[x] = dot_[x]
         delta[x] = jnp.sum(attn[x].astype(F32) * dot_[x].astype(F32), axis=0, keepdims=True)
         return carry
 
     lax.fori_loop(0, TILES, prepare, 0)
-    w1[TILES] = jnp.zeros((128, 2 * HALF), BF16)
+    gt[TILES] = jnp.zeros((64, HALF), BF16)
     delta[TILES] = jnp.zeros((1, HALF), F32)
     dkv[...] = jnp.zeros(dkv.shape, F32)
     if dq_in is None:
         dq[...] = jnp.zeros(dq.shape, F32)
     else:
         dq[...] = dq_in[...]
-
-    def scores(i, dst_a, dst_c):
-        band = kv[plan[2, i]]
-        dst_a[...] = dot(band, w1[plan[0, i]])
-        dst_c[...] = dot(band, w1[plan[1, i]])
-
-    def absorb(i, src_a, src_c):
+    blank = jnp.zeros((64, 2 * HALF), BF16)
+
+    def pair(ref, i):
+        return jnp.concatenate([ref[plan[0, i]], ref[plan[1, i]]], axis=1)
+
+    def scores(i, s, t, weigh=None):
+        wq = jnp.concatenate([pair(qt, i), blank], axis=0)
+        wg = jnp.concatenate([blank, pair(gt, i)], axis=0)
+        for low in range(0, rows, BACK_SUB):
+            at = slice(low, low + BACK_SUB)
+            band = kv[plan[2, i], at, :]
+            s[at, :] = dot(band, wq)
+            t[at, :] = dot(band, wg)
+            if weigh is not None:
+                weigh(at)
+
+    def weigh(i, s, t, p_ref, d_ref, at):
+        p = jnp.exp(s[at, :] - pair(lse, i))
+        p_ref[at, :] = p.astype(BF16)
+        d_ref[at, :] = (p * (t[at, :] - pair(delta, i))).astype(BF16)
+
+    def gather(i, p_ref, d_ref):
         a, c, b = plan[0, i], plan[1, i], plan[2, i]
-        both = []
-        for x, src in ((a, src_a), (c, src_c)):
-            p = jnp.exp(src[:, :HALF] - lse[x])
-            ds = p * (src[:, HALF:] - delta[x])
-            both.append((ds.astype(BF16), p.astype(BF16)))
-        (ds_a, p_a), (ds_c, p_c) = both
-        dkv[b] += dot(
-            jnp.concatenate([ds_a, p_a, ds_c, p_c], axis=1),
-            jnp.concatenate([w1[a], w1[c]], axis=1),
-            NT,
-        )
-        part = dot(kt[b], jnp.concatenate([ds_a, ds_c], axis=1))
+        part = dot(kt[b], d_ref[...])
         dq[a] += part[:, :HALF]
         dq[c] += part[:, HALF:]
-
-    scores(0, a0, c0)
-
-    def two(j, carry):
-        scores(2 * j + 1, a1, c1)
-        absorb(2 * j, a0, c0)
-        scores(2 * j + 2, a0, c0)
-        absorb(2 * j + 1, a1, c1)
+        dkv[b, :64, :] += dot(pair(qt, i), d_ref[...], NT)
+        dkv[b, 64:, :] += dot(pair(gt, i), p_ref[...], NT)
+
+    scores(0, s0, t0)
+    scores(1, s1, t1)
+    weigh(0, s0, t0, p0, d0, slice(0, rows))
+
+    even, odd = (s0, t0, p0, d0), (s1, t1, p1, d1)
+
+    def step(j, carry):
+        for k in range(BACK_UNROLL):
+            i = BACK_UNROLL * j + k
+            now, later = (even, odd) if k % 2 == 0 else (odd, even)
+            scores(i + 2, *now[:2], functools.partial(weigh, i + 1, *later))
+            gather(i, *now[2:])
         return carry
 
-    lax.fori_loop(0, plan[3, 0], two, 0)
+    lax.fori_loop(0, (plan[3, 0] + BACK_UNROLL - 1) // BACK_UNROLL, step, 0)
 
     first = QUERY_ROWS if last else 0
 
     def finish(b, carry):
-        send_ref[b, first : first + rows, :] = dkv[b].astype(BF16)
+        for j in range(rows // 128):
+            at = first + j * 128
+            send_ref[b, at : at + 128, :] = dkv[b, :, j * 128 : j * 128 + 128].astype(BF16)
         if last:
             for t in range(TILES_DEV):
                 send_ref[b, t * 64 : t * 64 + 64, :] = (dq[b * TILES_DEV + t] * SCALE).astype(BF16)
@@ -330,12 +366,13 @@
         out_specs=out_specs,
         out_shape=out_shape,
         scratch_shapes=[
-            pltpu.VMEM((TILES + 1, 128, 2 * HALF), BF16),
+            pltpu.VMEM((TILES + 1, 64, HALF), BF16),
             pltpu.VMEM((TILES + 1, 1, HALF), F32),
-            pltpu.VMEM((BANDS, ROWS, 128), F32),
+            pltpu.VMEM((BANDS, 128, ROWS), F32),
             pltpu.VMEM((TILES + 1, 64, HALF), F32),
         ]
-        + [pltpu.VMEM((ROWS, 2 * HALF), F32)] * 4,
+        + [pltpu.VMEM((ROWS, 2 * HALF), F32)] * 4
+        + [pltpu.VMEM((ROWS, 2 * HALF), BF16)] * 4,
         compiler_params=params(60),
         cost_estimate=cost(5e10 / CHUNKS, 2e7, 16e6 / CHUNKS),
         name="backward",
@@ -430,13 +467,14 @@
                 blocks.append(end[2 * head + half, t * 64 : t * 64 + 64, :])
         heads.append(jnp.concatenate(blocks, axis=1))
     dq_ref[...] = jnp.concatenate(heads, axis=0).T
-    left = lax.broadcasted_iota(jnp.int32, (ROWS, 128), 1) < 64
     for chunk, part, low in ((0, mid, 0), (1, end, QUERY_ROWS)):
-        take = [part[r, low : low + ROWS, :].astype(F32) for r in range(4)]
-        x, y = take[0] + take[1], take[2] + take[3]
-        at = slice(chunk * ROWS, chunk * ROWS + ROWS)
-        dk_ref[at, :] = jnp.where(left, x, pltpu.roll(y, 64, 1)).astype(BF16)
-        dv_ref[at, :] = jnp.where(left, pltpu.roll(x, 64, 1), y).astype(BF16)
+        for j in range(ROWS // 128):
+            block = slice(low + j * 128, low + j * 128 + 128)
+            take = [part[r, block, :].astype(F32) for r in range(4)]
+            x, y = take[0] + take[1], take[2] + take[3]
+            at = slice(chunk * ROWS + j * 128, chunk * ROWS + j * 128 + 128)
+            dk_ref[at, :] = jnp.concatenate([x[:64], y[:64]], axis=0).astype(BF16).T
+            dv_ref[at, :] = jnp.concatenate([x[64:], y[64:]], axis=0).astype(BF16).T
     for r in range(4):
         for j in range(D // 128):
             at = END_ROWS - DW_ROWS + j * 32

time: 269 us -> 235 us (0.87)
  Pallas kernels: 134 us -> 104 us
  blocking collectives: 62.8 us -> 57 us
    pallas_call x2, Pallas kernels: 69.3 us -> 53.4 us  [backward(): pl.pallas_call(body, grid=(1,), in_specs=specs, out_specs=out_specs, out_...]
    pallas_call x1, Pallas kernels: 41.2 us -> 27.2 us  [forward(): pl.pallas_call(forward_body, grid=(1,), in_specs=[SMEM, whole(16, SEND_RO...]
    all_to_all x2, blocking collectives: 62.8 us -> 57 us  [swap(): return lax.all_to_all(x, axes, 0, 0, tiled=True)]
  transfers between devices with their start and end apart: 4 -> 4, of which waited for: 1 -> 1; matrix products, arithmetic and copies ran while one was open for 0% -> 1% of each run, Pallas kernels for 43% -> 37%
where the time goes in v3:
time: 235 us; the launch traced here: 233 us
  Pallas kernels  104 us (44%)
  blocking collectives  57 us (24%)
  waiting for transfers between devices  35.2 us (15%)
  starting transfers between devices  29 us (12%)
  other arithmetic  4.23 us (2%)
  local copies, waits for them, and re-layouts  3.21 us (1%)
    all_to_all x2, blocking collectives, swap(): return lax.all_to_all(x, axes, 0, 0, tiled=True)  57 us
    pallas_call x2, Pallas kernels, backward(): pl.pallas_call(body, grid=(1,), in_specs=specs, out_specs=out_specs, out_...  53.4 us
    all_to_all x4, waiting for transfers between devices, swap(): return lax.all_to_all(x, axes, 0, 0, tiled=True)  35.2 us
    all_to_all x4, starting transfers between devices, swap(): return lax.all_to_all(x, axes, 0, 0, tiled=True)  29 us
    pallas_call x1, Pallas kernels, forward(): pl.pallas_call(forward_body, grid=(1,), in_specs=[SMEM, whole(16, SEND_RO...  27.2 us
    pallas_call x1, Pallas kernels, project(): pl.pallas_call(project_body, grid=(TILES_DEV,), in_specs=[pl.BlockSpec((1...  5.9 us
    pallas_call x1, Pallas kernels, dattn(): pl.pallas_call(dattn_body, grid=(4,), in_specs=[pl.BlockSpec((128, D), la...  5.2 us
  transfers between devices with their start and end apart: 4, of which 1 were waited for; matrix products, arithmetic and copies ran while one was open for 1% of the time, Pallas kernels for 37%

profile of v3, /device:TPU:0, one launch (start us, length us, event | category | flops | bytes accessed | tf_op | source)
XLA Modules:
  0.0 233.2 jit_solution(7060862674920212156)
XLA Ops:
  0.6 0.7 convert_bitcast_fusion.1
  1.4 0.7 convert.10
  2.3 0.6 pad.4.list_ref
  2.9 4.3 %pack.1 = bf16[16,720,128]{2,1,0:T(8,128)(2,1)} custom-call(bf16[768,512]{1,0:T(8,128)(2,1)} %bitcast.35, bf16[512,512]{1,0:T(8,128)(2,1)} %bitcast.36, bf16[512,512]{1,0:T(8,128)(2,1)} %bitcast.37, bf16[16,128]{1,0:T(8,128)(2,1)} %pad.4.list_ref), custom_call_target="tpu_custom_call" | custom-call | bytes 8000000 | tf_op jit(solution)/shard_map/pack/pallas_call | solution.py:81
  7.1 8.0 %all-to-all-start = ((bf16[16,720,128]{2,1,0:T(8,128)(2,1)}), bf16[16,720,128]{2,1,0:T(8,128)(2,1)S(1)}, u32[]{:S(2)}, u32[]{:S(2)}) async-start(bf16[16,720,128]{2,1,0:T(8,128)(2,1)} %pack.1), calls=%async_computation | async-start | bytes 5898240 | tf_op jit(solution)/shard_map/all_to_all | solution.py:512
  15.1 5.2 %dattn.1 = bf16[16,192,128]{2,1,0:T(8,128)(2,1)} custom-call(bf16[512,1024]{1,0:T(8,128)(2,1)} %w_ref.3, bf16[768,1024]{1,0:T(8,128)(2,1)} %bitcast.32), custom_call_target="tpu_custom_call" | custom-call | flops 805306368 | bytes 4000000 | tf_op jit(solution)/shard_map/dattn/pallas_call | solution.py:111
  20.3 35.2 %all-to-all-done.recv = bf16[16,720,128]{2,1,0:T(8,128)(2,1)S(1)} async-done(((bf16[16,720,128]{2,1,0:T(8,128)(2,1)}), bf16[16,720,128]{2,1,0:T(8,128)(2,1)S(1)}, u32[]{:S(2)}, u32[]{:S(2)}) %all-to-all-start) | async-done | bytes 2949152 | tf_op jit(solution)/shard_map/all_to_all | solution.py:512
  56.0 1.0 fusion.4
  57.2 0.2 reduce_window_sum.18
  57.5 0.3 select_reduce_fusion
  58.0 6.7 %all-to-all-start.2 = ((bf16[16,192,128]{2,1,0:T(8,128)(2,1)}), bf16[16,192,128]{2,1,0:T(8,128)(2,1)}, u32[]{:S(2)}, u32[]{:S(2)}) async-start(bf16[16,192,128]{2,1,0:T(8,128)(2,1)} %dattn.1), calls=%async_computation.2 | async-start | bytes 1572864 | tf_op jit(solution)/shard_map/all_to_all | solution.py:512
  64.7 0.7 pad.8.clone
  65.6 0.7 add_add_fusion.1.plan.refs_0_
  66.3 27.2 %forward.1 = (bf16[48,64,128]{2,1,0:T(8,128)(2,1)}, f32[49,1,128]{2,1,0:T(1,128)}, bf16[16,512,128]{2,1,0:T(8,128)(2,1)}, bf16[16,64,512]{2,1,0:T(8,128)(2,1)}, bf16[49,64,128]{2,1,0:T(8,128)(2,1)}) custom-call(s32[4,208]{1,0:T(4,128)} %add_add_fusion.1.plan.refs_0_, bf16[16,720,128]{2,1,0:T(8,128)(2,1)} %copy-done.1), custom_call_target="tpu_custom_call" | custom-call | flops 24000000000 | bytes 20000000 | tf_op jit(solution)/shard_map/forward/pallas_call | solution.py:218
  93.5 7.2 %all-to-all-start.1 = ((bf16[16,192,128]{2,1,0:T(8,128)(2,1)}), bf16[16,192,128]{2,1,0:T(8,128)(2,1)S(1)}, u32[]{:S(2)}, u32[]{:S(2)}) async-start(bf16[16,192,128]{2,1,0:T(8,128)(2,1)} %bitcast.34), calls=%async_computation.1 | async-start | bytes 1572864 | tf_op jit(solution)/shard_map/all_to_all | solution.py:512
  100.7 26.5 %backward.2 = (bf16[16,512,128]{2,1,0:T(8,128)(2,1)}, f32[49,64,128]{2,1,0:T(8,128)}) custom-call(s32[4,208]{1,0:T(4,128)} %add_add_fusion.1.plan.refs_0_, bf16[16,512,128]{2,1,0:T(8,128)(2,1)} %get-tuple-element.28.refs_1_, bf16[16,64,512]{2,1,0:T(8,128)(2,1)} %get-tuple-element.29.refs_2_, bf16[49,64,128]{2,1,0:T(8,128)(2,1)} %get-tuple-element.30.refs_3_, ...), custom_call_target="tpu_custom_call" | custom-call | flops 24999999488 | bytes 20000000 | tf_op jit(solution)/shard_map/backward/pallas_call | solution.py:362
  127.2 0.9 copy-done.2
  128.1 5.9 %project.1 = (bf16[768,1024]{1,0:T(8,128)(2,1)}, bf16[16,512,128]{2,1,0:T(8,128)(2,1)}) custom-call(bf16[16,192,128]{2,1,0:T(8,128)(2,1)} %copy-done.2, bf16[512,1024]{1,0:T(8,128)(2,1)} %w_ref.3, bf16[768,1024]{1,0:T(8,128)(2,1)} %bitcast.33, bf16[16,512,128]{2,1,0:T(8,128)(2,1)} %get-tuple-element.35.unused), custom_call_target="tpu_custom_call", output_to_operand_aliasing={{1}: (3, {})} | custom-call | flops 1610612736 | bytes 8000000 | tf_op jit(solution)/shard_map/project/pallas_call | solution.py:413
  134.0 7.2 %all-to-all-start.3 = ((bf16[16,512,128]{2,1,0:T(8,128)(2,1)}), bf16[16,512,128]{2,1,0:T(8,128)(2,1)S(1)}, u32[]{:S(2)}, u32[]{:S(2)}) async-start(bf16[16,512,128]{2,1,0:T(8,128)(2,1)} %get-tuple-element.39), calls=%async_computation.3 | async-start | bytes 4194304 | tf_op jit(solution)/shard_map/all_to_all | solution.py:512
  141.2 26.8 %backward.3.unused = bf16[16,704,128]{2,1,0:T(8,128)(2,1)} custom-call(s32[4,208]{1,0:T(4,128)} %add_add_fusion.1.plan.refs_0_, bf16[16,512,128]{2,1,0:T(8,128)(2,1)} %get-tuple-element.28.refs_1_, bf16[16,64,512]{2,1,0:T(8,128)(2,1)} %get-tuple-element.29.refs_2_, bf16[49,64,128]{2,1,0:T(8,128)(2,1)} %get-tuple-element.30.refs_3_, ...), custom_call_target="tpu_custom_call" | custom-call | flops 24999999488 | bytes 20000000 | tf_op jit(solution)/shard_map/backward/pallas_call | solution.py:362
  168.3 14.0 %all_to_all.30.part_ref = bf16[8,256,128]{2,1,0:T(8,128)(2,1)} all-to-all(bf16[8,256,128]{2,1,0:T(8,128)(2,1)S(1)} %broadcast_in_dim.39), channel_id=1, replica_groups=mesh['region'=16,'orbit'=8] {'orbit'}, dimensions={0} | all-to-all | bytes 1048576 | tf_op jit(solution)/shard_map/all_to_all | solution.py:512
  182.3 3.3 %spread.1 = bf16[16,704,128]{2,1,0:T(8,128)(2,1)} custom-call(bf16[8,256,128]{2,1,0:T(8,128)(2,1)} %all_to_all.30.part_ref, bf16[16,704,128]{2,1,0:T(8,128)(2,1)} %backward.3.unused), custom_call_target="tpu_custom_call", output_to_operand_aliasing={{}: (1, {})} | custom-call | bytes 2000000 | tf_op jit(solution)/shard_map/spread/pallas_call | solution.py:445
  185.6 43.0 %all_to_all.31.end = bf16[16,704,128]{2,1,0:T(8,128)(2,1)} all-to-all(bf16[16,704,128]{2,1,0:T(8,128)(2,1)} %spread.1), channel_id=1, replica_groups=mesh['region'=16,'orbit'=8] {'region'}, dimensions={0} | all-to-all | bytes 5767168 | tf_op jit(solution)/shard_map/all_to_all | solution.py:512
  228.6 4.6 %unpack.1 = (bf16[768,512]{1,0:T(8,128)(2,1)}, bf16[512,512]{1,0:T(8,128)(2,1)}, bf16[512,512]{1,0:T(8,128)(2,1)}, f32[512,1024]{1,0:T(8,128)}) custom-call(bf16[16,512,128]{2,1,0:T(8,128)(2,1)} %copy-done, bf16[16,704,128]{2,1,0:T(8,128)(2,1)} %all_to_all.31.end), custom_call_target="tpu_custom_call" | custom-call | bytes 8000000 | tf_op jit(solution)/shard_map/unpack/pallas_call | solution.py:486
  (33 shorter events, 1.8 us)
Async XLA Ops:
  7.1 48.3 %all-to-all-start = ((bf16[16,720,128]{2,1,0:T(8,128)(2,1)}), bf16[16,720,128]{2,1,0:T(8,128)(2,1)S(1)}, u32[]{:S(2)}, u32[]{:S(2)}) async-start(bf16[16,720,128]{2,1,0:T(8,128)(2,1)} %pack.1), calls=%async_computation | async-start | bytes 5898240 | tf_op jit(solution)/shard_map/all_to_all | solution.py:512
  55.5 10.9 %copy-start.1 = (bf16[16,720,128]{2,1,0:T(8,128)(2,1)}, bf16[16,720,128]{2,1,0:T(8,128)(2,1)S(1)}, u32[]{:S(2)}) copy-start(bf16[16,720,128]{2,1,0:T(8,128)(2,1)S(1)} %all-to-all-done.recv) | copy-start | bytes 8847364
  58.0 35.5 %all-to-all-start.2 = ((bf16[16,192,128]{2,1,0:T(8,128)(2,1)}), bf16[16,192,128]{2,1,0:T(8,128)(2,1)}, u32[]{:S(2)}, u32[]{:S(2)}) async-start(bf16[16,192,128]{2,1,0:T(8,128)(2,1)} %dattn.1), calls=%async_computation.2 | async-start | bytes 1572864 | tf_op jit(solution)/shard_map/all_to_all | solution.py:512
  93.5 33.7 %all-to-all-start.1 = ((bf16[16,192,128]{2,1,0:T(8,128)(2,1)}), bf16[16,192,128]{2,1,0:T(8,128)(2,1)S(1)}, u32[]{:S(2)}, u32[]{:S(2)}) async-start(bf16[16,192,128]{2,1,0:T(8,128)(2,1)} %bitcast.34), calls=%async_computation.1 | async-start | bytes 1572864 | tf_op jit(solution)/shard_map/all_to_all | solution.py:512
  127.2 0.9 copy-start.2
  134.0 34.1 %all-to-all-start.3 = ((bf16[16,512,128]{2,1,0:T(8,128)(2,1)}), bf16[16,512,128]{2,1,0:T(8,128)(2,1)S(1)}, u32[]{:S(2)}, u32[]{:S(2)}) async-start(bf16[16,512,128]{2,1,0:T(8,128)(2,1)} %get-tuple-element.39), calls=%async_computation.3 | async-start | bytes 4194304 | tf_op jit(solution)/shard_map/all_to_all | solution.py:512
  168.1 17.5 %copy-start = (bf16[16,512,128]{2,1,0:T(8,128)(2,1)}, bf16[16,512,128]{2,1,0:T(8,128)(2,1)S(1)}, u32[]{:S(2)}) copy-start(bf16[16,512,128]{2,1,0:T(8,128)(2,1)S(1)} %all-to-all-done.3.mid) | copy-start | bytes 6291460

commit v4 on v3

--- a/solution.py
+++ b/solution.py
@@ -30,7 +30,7 @@
 SEND_ROWS = LIST_ROW + 16
 DW_ROWS = HW * D // 16 // 128
 MID_ROWS = ROWS + DW_ROWS
-END_ROWS = QUERY_ROWS + ROWS + DW_ROWS
+END_ROWS = QUERY_ROWS + ROWS
 PAIRS = 208
 SCALE = HEAD_DIM**-0.5
 LOW = -1e30
@@ -59,7 +59,11 @@
 SMEM = pl.BlockSpec(memory_space=pltpu.SMEM)
 
 
-def pack_body(q_ref, k_ref, v_ref, list_ref, out_ref):
+def pack_body(q_ref, k_ref, v_ref, list_ref, count_ref, out_ref, rows_ref):
+    rows_ref[...] = jnp.zeros(rows_ref.shape, F32)
+    rows_ref[:TILES_DEV, :MAXB] = list_ref[...].astype(F32)
+    rows_ref[8:9, :TILES_DEV] = count_ref[...].astype(F32)
+    lists = rows_ref[...].astype(BF16)
     kt = k_ref[...].T
     vt = v_ref[...].T
     qt = (q_ref[...].astype(F32) * SCALE).astype(BF16).T
@@ -67,7 +71,7 @@
         rows = slice(head * 64, head * 64 + 64)
         for half in range(2):
             dest = 2 * head + half
-            out_ref[dest, LIST_ROW:SEND_ROWS, :] = list_ref[...]
+            out_ref[dest, LIST_ROW:SEND_ROWS, :] = lists
             for j in range(4):
                 lanes = slice(j * 128, j * 128 + 128)
                 out_ref[dest, j * 128 : j * 128 + 64, :] = kt[rows, lanes]
@@ -77,7 +81,7 @@
                 out_ref[dest, BT + t * 64 : BT + t * 64 + 64, :] = qt[rows, low : low + HALF]
 
 
-def pack(q, k, v, lists):
+def pack(q, k, v, lists, counts):
     return pl.pallas_call(
         pack_body,
         grid=(4,),
@@ -85,14 +89,16 @@
             pl.BlockSpec((TILES_DEV * QROWS, 128), lambda p: (0, p)),
             pl.BlockSpec((BT, 128), lambda p: (0, p)),
             pl.BlockSpec((BT, 128), lambda p: (0, p)),
-            pl.BlockSpec((16, 128), lambda p: (0, 0)),
+            pl.BlockSpec((TILES_DEV, MAXB), lambda p: (0, 0)),
+            pl.BlockSpec((1, TILES_DEV), lambda p: (0, 0)),
         ],
         out_specs=pl.BlockSpec((4, SEND_ROWS, 128), lambda p: (p, 0, 0)),
         out_shape=jax.ShapeDtypeStruct((16, SEND_ROWS, 128), BF16),
+        scratch_shapes=[pltpu.VMEM((16, 128), F32)],
         compiler_params=params(60),
         cost_estimate=cost(0, 8e6),
         name="pack",
-    )(q, k, v, lists)
+    )(q, k, v, lists, counts)
 
 
 def dattn_body(w_ref, g_ref, out_ref):
@@ -379,86 +385,67 @@
     )(*args)
 
 
-def project_body(recv, w_ref, g_ref, unused, layer_ref, send_ref, acc):
-    t = pl.program_id(0)
-    low = pl.multiple_of(t * 64, 64)
+def attn_columns(recv, low):
     heads = [
         jnp.concatenate([recv[2 * h, pl.ds(low, 64), :], recv[2 * h + 1, pl.ds(low, 64), :]], axis=1)
         for h in range(HEADS)
     ]
-    attn_t = jnp.concatenate(heads, axis=0)
-    layer_ref[...] = dot(attn_t.T, w_ref[...]).astype(BF16)
-    term = dot(attn_t, g_ref[...])
-
-    @pl.when(t == 0)
-    def _():
-        acc[...] = term
-
-    @pl.when(t > 0)
-    def _():
-        acc[...] += term
-
-    @pl.when(t == TILES_DEV - 1)
-    def _():
-        wide = D // 128
-        for dest in range(16):
-            for j in range(wide):
-                send_ref[dest, j * 32 : j * 32 + 32, :] = acc[
-                    dest * 32 : dest * 32 + 32, j * 128 : j * 128 + 128
-                ].astype(BF16)
-
-
-def project(recv, w, g, send):
+    return jnp.concatenate(heads, axis=0)
+
+
+def weight_body(recv, g_ref, unused, send_ref):
+    g = g_ref[...]
+    for t in range(TILES_DEV):
+        term = dot(attn_columns(recv, t * 64), g[t * QROWS : (t + 1) * QROWS])
+        total = term if t == 0 else total + term
+    total = total.astype(BF16)
+    for dest in range(16):
+        send_ref[dest] = total[dest * 32 : dest * 32 + 32]
+
+
+def weight_grad(recv, g, send):
     rows = TILES_DEV * QROWS
-    return pl.pallas_call(
-        project_body,
+    steps = D // 128
+    return pl.pallas_call(
+        weight_body,
+        grid=(steps,),
+        in_specs=[
+            pl.BlockSpec((16, QUERY_ROWS, 128), lambda j: (0, 0, 0)),
+            pl.BlockSpec((rows, 128), lambda j: (0, j)),
+            pl.BlockSpec(memory_space=pl.ANY),
+        ],
+        out_specs=pl.BlockSpec((16, 32, 128), lambda j: (0, ROWS // 32 + j, 0)),
+        out_shape=jax.ShapeDtypeStruct((BANDS, MID_ROWS, 128), BF16),
+        input_output_aliases={2: 0},
+        compiler_params=params(60),
+        cost_estimate=cost(2 * rows * D * HW, 5e6),
+        name="weight_grad",
+    )(recv, g, send)
+
+
+def layer_body(recv, w_ref, layer_ref):
+    low = pl.multiple_of(pl.program_id(0) * 64, 64)
+    layer_ref[...] = dot(attn_columns(recv, low).T, w_ref[...]).astype(BF16)
+
+
+def layer_output(recv, w):
+    rows = TILES_DEV * QROWS
+    return pl.pallas_call(
+        layer_body,
         grid=(TILES_DEV,),
         in_specs=[
-            pl.BlockSpec((16, TILES_DEV * 64, 128), lambda t: (0, 0, 0)),
+            pl.BlockSpec((16, QUERY_ROWS, 128), lambda t: (0, 0, 0)),
             pl.BlockSpec((HW, D), lambda t: (0, 0)),
-            pl.BlockSpec((QROWS, D), lambda t: (t, 0)),
-            pl.BlockSpec(memory_space=pl.ANY),
-        ],
-        out_specs=[
-            pl.BlockSpec((QROWS, D), lambda t: (t, 0)),
-            pl.BlockSpec((16, DW_ROWS, 128), lambda t: (0, ROWS // DW_ROWS, 0)),
-        ],
-        out_shape=[
-            jax.ShapeDtypeStruct((rows, D), BF16),
-            jax.ShapeDtypeStruct((BANDS, MID_ROWS, 128), BF16),
-        ],
-        input_output_aliases={3: 1},
-        scratch_shapes=[pltpu.VMEM((HW, D), F32)],
-        compiler_params=params(60),
-        cost_estimate=cost(4 * rows * D * HW, 8e6),
-        name="project",
-    )(recv, w, g, send)
-
-
-def spread_body(part_ref, unused, send_ref):
-    total = jnp.sum(part_ref[...].astype(F32), axis=0).astype(BF16)
-    for dest in range(16):
-        send_ref[dest] = total
-
-
-def spread(part, send):
-    return pl.pallas_call(
-        spread_body,
-        grid=(DW_ROWS // 64,),
-        in_specs=[
-            pl.BlockSpec((part.shape[0], 64, 128), lambda i: (0, i, 0)),
-            pl.BlockSpec(memory_space=pl.ANY),
-        ],
-        out_specs=pl.BlockSpec((16, 64, 128), lambda i: (0, (END_ROWS - DW_ROWS) // 64 + i, 0)),
-        out_shape=jax.ShapeDtypeStruct((BANDS, END_ROWS, 128), BF16),
-        input_output_aliases={1: 0},
-        compiler_params=params(60),
-        cost_estimate=cost(0, 2e6),
-        name="spread",
-    )(part, send)
-
-
-def unpack_body(mid, end, dq_ref, dk_ref, dv_ref, dw_ref):
+        ],
+        out_specs=pl.BlockSpec((QROWS, D), lambda t: (t, 0)),
+        out_shape=jax.ShapeDtypeStruct((rows, D), BF16),
+        compiler_params=params(60),
+        cost_estimate=cost(2 * rows * D * HW, 4e6),
+        name="layer_output",
+    )(recv, w)
+
+
+def unpack_body(mid, end, dq_ref, dk_ref, dv_ref):
     heads = []
     for head in range(2):
         blocks = []
@@ -475,10 +462,27 @@
             at = slice(chunk * ROWS + j * 128, chunk * ROWS + j * 128 + 128)
             dk_ref[at, :] = jnp.concatenate([x[:64], y[:64]], axis=0).astype(BF16).T
             dv_ref[at, :] = jnp.concatenate([x[64:], y[64:]], axis=0).astype(BF16).T
+
+
+def weight_out_body(part, dw_ref):
     for r in range(4):
         for j in range(D // 128):
-            at = END_ROWS - DW_ROWS + j * 32
-            dw_ref[r * 32 : r * 32 + 32, j * 128 : j * 128 + 128] = end[r, at : at + 32, :].astype(F32)
+            dw_ref[r * 32 : r * 32 + 32, j * 128 : j * 128 + 128] = part[
+                r, j * 32 : j * 32 + 32, :
+            ].astype(F32)
+
+
+def weight_out(part):
+    return pl.pallas_call(
+        weight_out_body,
+        grid=(4,),
+        in_specs=[pl.BlockSpec((4, DW_ROWS, 128), lambda p: (p, 0, 0))],
+        out_specs=pl.BlockSpec((128, D), lambda p: (p, 0)),
+        out_shape=jax.ShapeDtypeStruct((HW, D), F32),
+        compiler_params=params(60),
+        cost_estimate=cost(0, 3e6),
+        name="weight_out",
+    )(part)
 
 
 def unpack(mid, end):
@@ -494,13 +498,11 @@
             pl.BlockSpec((rows, 128), lambda p: (0, p)),
             pl.BlockSpec((BT, 128), lambda p: (0, p)),
             pl.BlockSpec((BT, 128), lambda p: (0, p)),
-            pl.BlockSpec((128, D), lambda p: (p, 0)),
         ],
         out_shape=[
             jax.ShapeDtypeStruct((rows, HW), BF16),
             jax.ShapeDtypeStruct((BT, HW), BF16),
             jax.ShapeDtypeStruct((BT, HW), BF16),
-            jax.ShapeDtypeStruct((HW, D), F32),
         ],
         compiler_params=params(60),
         cost_estimate=cost(0, 8e6),
@@ -512,15 +514,22 @@
     return lax.all_to_all(x, axes, 0, 0, tiled=True)
 
 
+def orbit_sum(share):
+    size = lax.axis_size("orbit")
+    total = share.astype(F32)
+    for shift in range(1, size):
+        total += lax.ppermute(share, "orbit", [(i, (i + shift) % size) for i in range(size)]).astype(F32)
+    return total
+
+
 def per_device(queries, keys, values, block_lists, band_counts, cotangent, out_weight):
     rows = TILES_DEV * QROWS
     q, g = queries.reshape(rows, HW), cotangent.reshape(rows, D)
-    lists = jnp.concatenate([block_lists[0], band_counts[0][:, None]], axis=1).astype(BF16)
-    lists = lists.reshape(1, -1)
-    lists = jnp.pad(lists, ((0, 15), (0, 128 - lists.shape[1])))
-    recv = swap(pack(q, keys.reshape(BT, HW), values.reshape(BT, HW), lists))
-    lists = recv[:, LIST_ROW, : TILES_DEV * (MAXB + 1)].astype(jnp.int32).reshape(TILES, MAXB + 1)
-    plan = plan_of(lists[:, :MAXB], lists[:, MAXB])
+    k, v = keys.reshape(BT, HW), values.reshape(BT, HW)
+    recv = swap(pack(q, k, v, block_lists[0], band_counts))
+    lists = recv[:, LIST_ROW : LIST_ROW + TILES_DEV, :MAXB].astype(jnp.int32).reshape(TILES, MAXB)
+    counts = recv[:, LIST_ROW + 8, :TILES_DEV].astype(jnp.int32).reshape(TILES)
+    plan = plan_of(lists, counts)
     d_attn = dattn(out_weight, g)
     recv, d_attn = lax.optimization_barrier((recv, d_attn))
     d_attn = swap(d_attn).reshape(TILES, 64, HALF)
@@ -529,22 +538,24 @@
     attn_home = swap(attn.reshape(16, QUERY_ROWS, HALF))
     mid, dq = backward(0, plan, kv, kt, qt, d_attn, attn, lse)
     attn_home, mid = lax.optimization_barrier((attn_home, mid))
-    layer, mid = project(attn_home, out_weight, g, mid)
+    mid = weight_grad(attn_home, g, mid)
     mid, dq = lax.optimization_barrier((mid, dq))
     mid = swap(mid)
     (end,) = backward(1, plan, kv, kt, qt, d_attn, attn, lse, dq)
-    mid, end = lax.optimization_barrier((mid, end))
-    share = jnp.sum(mid[:, ROWS:].astype(F32), axis=0, keepdims=True).astype(BF16)
-    orbits = lax.axis_size("orbit")
-    share = swap(jnp.broadcast_to(share, (orbits, DW_ROWS, 128)), "orbit")
-    end = swap(spread(share, end))
-    d_q, d_k, d_v, d_weight = unpack(mid, end)
+    mid, end, attn_home = lax.optimization_barrier((mid, end, attn_home))
+    end = swap(end)
+    share = jnp.sum(mid[:, ROWS:].astype(F32), axis=0).astype(BF16)
+    total = orbit_sum(share).astype(BF16)
+    layer = layer_output(attn_home, out_weight)
+    end, total, layer = lax.optimization_barrier((end, total, layer))
+    total = swap(jnp.broadcast_to(total[None], (16, DW_ROWS, 128)))
+    d_q, d_k, d_v = unpack(mid, end)
     return (
         layer.reshape(1, TILES_DEV, QROWS, D),
         d_q.reshape(1, TILES_DEV, QROWS, HW),
         d_k.reshape(1, 1, BT, HW),
         d_v.reshape(1, 1, BT, HW),
-        d_weight,
+        weight_out(total),
     )
 
 

time: 235 us -> 221 us (0.940)
  blocking collectives: 57 us -> 0 us
  waiting for transfers between devices: 35.2 us -> 57 us
  starting transfers between devices: 29 us -> 48.4 us
  local copies, waits for them, and re-layouts: 3.21 us -> 5.63 us
    all_to_all x2 -> x0, blocking collectives: 57 us -> none  [swap(): return lax.all_to_all(x, axes, 0, 0, tiled=True)]
    all_to_all x4 -> x6, waiting for transfers between devices: 35.2 us -> 55.3 us  [swap(): return lax.all_to_all(x, axes, 0, 0, tiled=True)]
    ppermute x0 -> x7, starting transfers between devices: none -> 10.4 us  [orbit_sum(): lax.ppermute(share, 'orbit', [(i, (i + shift) % size) for i in range(size)])]
    all_to_all x4 -> x6, starting transfers between devices: 29 us -> 38 us  [swap(): return lax.all_to_all(x, axes, 0, 0, tiled=True)]
    pallas_call x2 -> x3, Pallas kernels: 9.22 us -> 14.6 us  [the longest x1 7.05 us: weight_grad(): pl.pallas_call(weight_body, grid=(steps,), in_specs=[pl.BlockSpec((16, QU...]
    pallas_call x2, Pallas kernels: 53.4 us -> 50.8 us  [backward(): pl.pallas_call(body, grid=(1,), in_specs=specs, out_specs=out_specs, out_...]
  transfers between devices with their start and end apart: 4 -> 13, of which waited for: 1 -> 6; matrix products, arithmetic and copies ran while one was open for 1% -> 1% of each run, Pallas kernels for 37% -> 41%
where the time goes in v4:
time: 221 us; the launch traced here: 220 us
  Pallas kernels  105 us (48%)
  waiting for transfers between devices  57 us (26%)
  starting transfers between devices  48.4 us (22%)
  local copies, waits for them, and re-layouts  5.63 us (3%)
  other arithmetic  2.92 us (1%)
    all_to_all x6, waiting for transfers between devices, swap(): return lax.all_to_all(x, axes, 0, 0, tiled=True)  55.3 us
    pallas_call x2, Pallas kernels, backward(): pl.pallas_call(body, grid=(1,), in_specs=specs, out_specs=out_specs, out_...  50.8 us
    all_to_all x6, starting transfers between devices, swap(): return lax.all_to_all(x, axes, 0, 0, tiled=True)  38 us
    pallas_call x1, Pallas kernels, forward(): pl.pallas_call(forward_body, grid=(1,), in_specs=[SMEM, whole(16, SEND_RO...  26 us
    ppermute x7, starting transfers between devices, orbit_sum(): lax.ppermute(share, 'orbit', [(i, (i + shift) % size) for i in range(size)])  10.4 us
    pallas_call x1, Pallas kernels, weight_grad(): pl.pallas_call(weight_body, grid=(steps,), in_specs=[pl.BlockSpec((16, QU...  7.05 us
    pallas_call x1, Pallas kernels, dattn(): pl.pallas_call(dattn_body, grid=(4,), in_specs=[pl.BlockSpec((128, D), la...  5.19 us
  transfers between devices with their start and end apart: 13, of which 6 were waited for; matrix products, arithmetic and copies ran while one was open for 1% of the time, Pallas kernels for 41%

profile of v4, /device:TPU:0, one launch (start us, length us, event | category | flops | bytes accessed | tf_op | source)
XLA Modules:
  0.0 219.6 jit_solution(14603884004797563015)
XLA Ops:
  0.6 1.3 copy.19
  1.9 4.3 %pack.1 = bf16[16,720,128]{2,1,0:T(8,128)(2,1)} custom-call(bf16[768,512]{1,0:T(8,128)(2,1)} %bitcast.32, bf16[512,512]{1,0:T(8,128)(2,1)} %bitcast.34, bf16[512,512]{1,0:T(8,128)(2,1)} %bitcast.35, s32[3,8]{1,0:T(4,128)} %bitcast.36, s32[1,3]{1,0:T(1,128)} %count_ref.1), custom_call_target="tpu_custom_call" | custom-call | bytes 8000000 | tf_op jit(solution)/shard_map/pack/pallas_call | solution.py:85
  6.2 8.0 %all-to-all-start = ((bf16[16,720,128]{2,1,0:T(8,128)(2,1)}), bf16[16,720,128]{2,1,0:T(8,128)(2,1)S(1)}, u32[]{:S(2)}, u32[]{:S(2)}) async-start(bf16[16,720,128]{2,1,0:T(8,128)(2,1)} %pack.1), calls=%async_computation | async-start | bytes 5898240 | tf_op jit(solution)/shard_map/all_to_all | solution.py:514
  14.1 5.2 %dattn.1 = bf16[16,192,128]{2,1,0:T(8,128)(2,1)} custom-call(bf16[512,1024]{1,0:T(8,128)(2,1)} %w_ref.3, bf16[768,1024]{1,0:T(8,128)(2,1)} %bitcast.29), custom_call_target="tpu_custom_call" | custom-call | flops 805306368 | bytes 4000000 | tf_op jit(solution)/shard_map/dattn/pallas_call | solution.py:117
  19.3 35.2 %all-to-all-done.recv = bf16[16,720,128]{2,1,0:T(8,128)(2,1)S(1)} async-done(((bf16[16,720,128]{2,1,0:T(8,128)(2,1)}), bf16[16,720,128]{2,1,0:T(8,128)(2,1)S(1)}, u32[]{:S(2)}, u32[]{:S(2)}) %all-to-all-start) | async-done | bytes 2949152 | tf_op jit(solution)/shard_map/all_to_all | solution.py:514
  57.0 6.7 %all-to-all-start.2 = ((bf16[16,192,128]{2,1,0:T(8,128)(2,1)}), bf16[16,192,128]{2,1,0:T(8,128)(2,1)}, u32[]{:S(2)}, u32[]{:S(2)}) async-start(bf16[16,192,128]{2,1,0:T(8,128)(2,1)} %dattn.1), calls=%async_computation.2 | async-start | bytes 1572864 | tf_op jit(solution)/shard_map/all_to_all | solution.py:514
  65.3 26.0 %forward.1 = (bf16[48,64,128]{2,1,0:T(8,128)(2,1)}, f32[49,1,128]{2,1,0:T(1,128)}, bf16[16,512,128]{2,1,0:T(8,128)(2,1)}, bf16[16,64,512]{2,1,0:T(8,128)(2,1)}, bf16[49,64,128]{2,1,0:T(8,128)(2,1)}) custom-call(s32[4,208]{1,0:T(4,128)} %add_add_fusion.1.plan.refs_0_, bf16[16,720,128]{2,1,0:T(8,128)(2,1)} %copy-done.3), custom_call_target="tpu_custom_call" | custom-call | flops 24000000000 | bytes 20000000 | tf_op jit(solution)/shard_map/forward/pallas_call | solution.py:224
  91.3 7.2 %all-to-all-start.1 = ((bf16[16,192,128]{2,1,0:T(8,128)(2,1)}), bf16[16,192,128]{2,1,0:T(8,128)(2,1)S(1)}, u32[]{:S(2)}, u32[]{:S(2)}) async-start(bf16[16,192,128]{2,1,0:T(8,128)(2,1)} %bitcast.33), calls=%async_computation.1 | async-start | bytes 1572864 | tf_op jit(solution)/shard_map/all_to_all | solution.py:514
  98.4 25.2 %backward.2 = (bf16[16,512,128]{2,1,0:T(8,128)(2,1)}, f32[49,64,128]{2,1,0:T(8,128)}) custom-call(s32[4,208]{1,0:T(4,128)} %add_add_fusion.1.plan.refs_0_, bf16[16,512,128]{2,1,0:T(8,128)(2,1)} %get-tuple-element.29.refs_1_, bf16[16,64,512]{2,1,0:T(8,128)(2,1)} %get-tuple-element.30.refs_2_, bf16[49,64,128]{2,1,0:T(8,128)(2,1)} %get-tuple-element.31.refs_3_, ...), custom_call_target="tpu_custom_call" | custom-call | flops 24999999488 | bytes 20000000 | tf_op jit(solution)/shard_map/backward/pallas_call | solution.py:368
  124.5 7.1 %weight_grad.1 = bf16[16,512,128]{2,1,0:T(8,128)(2,1)} custom-call(bf16[16,192,128]{2,1,0:T(8,128)(2,1)} %copy-done.1, bf16[768,1024]{1,0:T(8,128)(2,1)} %bitcast.30, bf16[16,512,128]{2,1,0:T(8,128)(2,1)} %get-tuple-element.36.unused), custom_call_target="tpu_custom_call", output_to_operand_aliasing={{}: (2, {})} | custom-call | flops 805306368 | bytes 5000000 | tf_op jit(solution)/shard_map/weight_grad/pallas_call | solution.py:409
  131.6 7.2 %all-to-all-start.3 = ((bf16[16,512,128]{2,1,0:T(8,128)(2,1)}), bf16[16,512,128]{2,1,0:T(8,128)(2,1)S(1)}, u32[]{:S(2)}, u32[]{:S(2)}) async-start(bf16[16,512,128]{2,1,0:T(8,128)(2,1)} %weight_grad.1), calls=%async_computation.3 | async-start | bytes 4194304 | tf_op jit(solution)/shard_map/all_to_all | solution.py:514
  138.8 25.6 %backward.3 = bf16[16,448,128]{2,1,0:T(8,128)(2,1)} custom-call(s32[4,208]{1,0:T(4,128)} %add_add_fusion.1.plan.refs_0_, bf16[16,512,128]{2,1,0:T(8,128)(2,1)} %get-tuple-element.29.refs_1_, bf16[16,64,512]{2,1,0:T(8,128)(2,1)} %get-tuple-element.30.refs_2_, bf16[49,64,128]{2,1,0:T(8,128)(2,1)} %get-tuple-element.31.refs_3_, ...), custom_call_target="tpu_custom_call" | custom-call | flops 24999999488 | bytes 20000000 | tf_op jit(solution)/shard_map/backward/pallas_call | solution.py:368
  164.4 2.1 all-to-all-done.3.mid
  166.4 5.2 %all-to-all-start.4 = ((bf16[16,448,128]{2,1,0:T(8,128)(2,1)}), bf16[16,448,128]{2,1,0:T(8,128)(2,1)}, u32[]{:S(2)}, u32[]{:S(2)}) async-start(bf16[16,448,128]{2,1,0:T(8,128)(2,1)} %backward.3), calls=%async_computation.4 | async-start | bytes 3670016 | tf_op jit(solution)/shard_map/all_to_all | solution.py:514
  171.8 3.1 %collective-permute-start.5 = (bf16[256,128]{1,0:T(8,128)(2,1)S(1)}, bf16[256,128]{1,0:T(8,128)(2,1)S(1)}, u32[]{:S(2)}, u32[]{:S(2)}) collective-permute-start(bf16[256,128]{1,0:T(8,128)(2,1)S(1)} %slice_reduce_fusion), channel_id=1, source_target_pairs={{0,6},{1,7},{2,0},{3,1},{4,2},{5,3},{6,4},{7,5},{8,14},{9,15},{10,... | collective-permute-start | bytes 196616 | tf_op jit(solution)/shard_map/ppermute | solution.py:521
  175.0 4.1 %collective-permute-start.4 = (bf16[256,128]{1,0:T(8,128)(2,1)S(1)}, bf16[256,128]{1,0:T(8,128)(2,1)S(1)}, u32[]{:S(2)}, u32[]{:S(2)}) collective-permute-start(bf16[256,128]{1,0:T(8,128)(2,1)S(1)} %slice_reduce_fusion), channel_id=1, source_target_pairs={{0,5},{1,6},{2,7},{3,0},{4,1},{5,2},{6,3},{7,4},{8,13},{9,14},{10,... | collective-permute-start | bytes 196616 | tf_op jit(solution)/shard_map/ppermute | solution.py:521
  181.3 1.4 collective-permute-start
  182.7 4.0 %layer_output.1 = bf16[768,1024]{1,0:T(8,128)(2,1)} custom-call(bf16[16,192,128]{2,1,0:T(8,128)(2,1)} %copy-done.1, bf16[512,1024]{1,0:T(8,128)(2,1)} %w_ref.3), custom_call_target="tpu_custom_call" | custom-call | flops 805306368 | bytes 4000000 | tf_op jit(solution)/shard_map/layer_output/pallas_call | solution.py:433
  188.0 6.9 %all-to-all-done.4.end = bf16[16,448,128]{2,1,0:T(8,128)(2,1)} async-done(((bf16[16,448,128]{2,1,0:T(8,128)(2,1)}), bf16[16,448,128]{2,1,0:T(8,128)(2,1)}, u32[]{:S(2)}, u32[]{:S(2)}) %all-to-all-start.4) | async-done | bytes 1835040 | tf_op jit(solution)/shard_map/all_to_all | solution.py:514
  194.9 1.2 broadcast_in_dim.38
  196.1 3.8 %all-to-all-start.5 = ((bf16[16,256,128]{2,1,0:T(8,128)(2,1)}), bf16[16,256,128]{2,1,0:T(8,128)(2,1)S(1)}, u32[]{:S(2)}, u32[]{:S(2)}) async-start(bf16[16,256,128]{2,1,0:T(8,128)(2,1)} %broadcast_in_dim.38), calls=%async_computation.5 | async-start | bytes 2097152 | tf_op jit(solution)/shard_map/all_to_all | solution.py:514
  199.9 4.0 %unpack.1 = (bf16[768,512]{1,0:T(8,128)(2,1)}, bf16[512,512]{1,0:T(8,128)(2,1)}, bf16[512,512]{1,0:T(8,128)(2,1)}) custom-call(bf16[16,512,128]{2,1,0:T(8,128)(2,1)} %copy-done, bf16[16,448,128]{2,1,0:T(8,128)(2,1)} %all-to-all-done.4.end), custom_call_target="tpu_custom_call" | custom-call | bytes 8000000 | tf_op jit(solution)/shard_map/unpack/pallas_call | solution.py:490
  203.9 11.1 %all-to-all-done.5.part = bf16[16,256,128]{2,1,0:T(8,128)(2,1)S(1)} async-done(((bf16[16,256,128]{2,1,0:T(8,128)(2,1)}), bf16[16,256,128]{2,1,0:T(8,128)(2,1)S(1)}, u32[]{:S(2)}, u32[]{:S(2)}) %all-to-all-start.5) | async-done | bytes 1048608 | tf_op jit(solution)/shard_map/all_to_all | solution.py:514
  216.0 3.6 %weight_out.1 = f32[512,1024]{1,0:T(8,128)} custom-call(bf16[16,256,128]{2,1,0:T(8,128)(2,1)} %copy-done.2), custom_call_target="tpu_custom_call" | custom-call | bytes 3000000 | tf_op jit(solution)/shard_map/weight_out/pallas_call | solution.py:476
  (48 shorter events, 9.6 us)
Async XLA Ops:
  6.2 48.3 %all-to-all-start = ((bf16[16,720,128]{2,1,0:T(8,128)(2,1)}), bf16[16,720,128]{2,1,0:T(8,128)(2,1)S(1)}, u32[]{:S(2)}, u32[]{:S(2)}) async-start(bf16[16,720,128]{2,1,0:T(8,128)(2,1)} %pack.1), calls=%async_computation | async-start | bytes 5898240 | tf_op jit(solution)/shard_map/all_to_all | solution.py:514
  54.5 10.8 %copy-start.3 = (bf16[16,720,128]{2,1,0:T(8,128)(2,1)}, bf16[16,720,128]{2,1,0:T(8,128)(2,1)S(1)}, u32[]{:S(2)}) copy-start(bf16[16,720,128]{2,1,0:T(8,128)(2,1)S(1)} %all-to-all-done.recv) | copy-start | bytes 8847364
  57.0 34.3 %all-to-all-start.2 = ((bf16[16,192,128]{2,1,0:T(8,128)(2,1)}), bf16[16,192,128]{2,1,0:T(8,128)(2,1)}, u32[]{:S(2)}, u32[]{:S(2)}) async-start(bf16[16,192,128]{2,1,0:T(8,128)(2,1)} %dattn.1), calls=%async_computation.2 | async-start | bytes 1572864 | tf_op jit(solution)/shard_map/all_to_all | solution.py:514
  91.3 32.4 %all-to-all-start.1 = ((bf16[16,192,128]{2,1,0:T(8,128)(2,1)}), bf16[16,192,128]{2,1,0:T(8,128)(2,1)S(1)}, u32[]{:S(2)}, u32[]{:S(2)}) async-start(bf16[16,192,128]{2,1,0:T(8,128)(2,1)} %bitcast.33), calls=%async_computation.1 | async-start | bytes 1572864 | tf_op jit(solution)/shard_map/all_to_all | solution.py:514
  123.7 0.9 copy-start.1
  131.6 34.9 %all-to-all-start.3 = ((bf16[16,512,128]{2,1,0:T(8,128)(2,1)}), bf16[16,512,128]{2,1,0:T(8,128)(2,1)S(1)}, u32[]{:S(2)}, u32[]{:S(2)}) async-start(bf16[16,512,128]{2,1,0:T(8,128)(2,1)} %weight_grad.1), calls=%async_computation.3 | async-start | bytes 4194304 | tf_op jit(solution)/shard_map/all_to_all | solution.py:514
  166.4 5.3 %copy-start = (bf16[16,512,128]{2,1,0:T(8,128)(2,1)}, bf16[16,512,128]{2,1,0:T(8,128)(2,1)S(1)}, u32[]{:S(2)}) copy-start(bf16[16,512,128]{2,1,0:T(8,128)(2,1)S(1)} %all-to-all-done.3.mid) | copy-start | bytes 6291460
  166.4 28.5 %all-to-all-start.4 = ((bf16[16,448,128]{2,1,0:T(8,128)(2,1)}), bf16[16,448,128]{2,1,0:T(8,128)(2,1)}, u32[]{:S(2)}, u32[]{:S(2)}) async-start(bf16[16,448,128]{2,1,0:T(8,128)(2,1)} %backward.3), calls=%async_computation.4 | async-start | bytes 3670016 | tf_op jit(solution)/shard_map/all_to_all | solution.py:514
  171.8 8.4 %collective-permute-start.6 = (bf16[256,128]{1,0:T(8,128)(2,1)S(1)}, bf16[256,128]{1,0:T(8,128)(2,1)S(1)}, u32[]{:S(2)}, u32[]{:S(2)}) collective-permute-start(bf16[256,128]{1,0:T(8,128)(2,1)S(1)} %slice_reduce_fusion), channel_id=1, source_target_pairs={{0,7},{1,0},{2,1},{3,2},{4,3},{5,4},{6,5},{7,6},{8,15},{9,8},{10,9... | collective-permute-start | bytes 196616 | tf_op jit(solution)/shard_map/ppermute | solution.py:521
  171.8 9.5 %collective-permute-start.5 = (bf16[256,128]{1,0:T(8,128)(2,1)S(1)}, bf16[256,128]{1,0:T(8,128)(2,1)S(1)}, u32[]{:S(2)}, u32[]{:S(2)}) collective-permute-start(bf16[256,128]{1,0:T(8,128)(2,1)S(1)} %slice_reduce_fusion), channel_id=1, source_target_pairs={{0,6},{1,7},{2,0},{3,1},{4,2},{5,3},{6,4},{7,5},{8,14},{9,15},{10,... | collective-permute-start | bytes 196616 | tf_op jit(solution)/shard_map/ppermute | solution.py:521
  175.0 11.7 %collective-permute-start.4 = (bf16[256,128]{1,0:T(8,128)(2,1)S(1)}, bf16[256,128]{1,0:T(8,128)(2,1)S(1)}, u32[]{:S(2)}, u32[]{:S(2)}) collective-permute-start(bf16[256,128]{1,0:T(8,128)(2,1)S(1)} %slice_reduce_fusion), channel_id=1, source_target_pairs={{0,5},{1,6},{2,7},{3,0},{4,1},{5,2},{6,3},{7,4},{8,13},{9,14},{10,... | collective-permute-start | bytes 196616 | tf_op jit(solution)/shard_map/ppermute | solution.py:521
  179.1 7.7 %collective-permute-start.3 = (bf16[256,128]{1,0:T(8,128)(2,1)S(1)}, bf16[256,128]{1,0:T(8,128)(2,1)S(1)}, u32[]{:S(2)}, u32[]{:S(2)}) collective-permute-start(bf16[256,128]{1,0:T(8,128)(2,1)S(1)} %slice_reduce_fusion), channel_id=1, source_target_pairs={{0,4},{1,5},{2,6},{3,7},{4,0},{5,1},{6,2},{7,3},{8,12},{9,13},{10,... | collective-permute-start | bytes 196616 | tf_op jit(solution)/shard_map/ppermute | solution.py:521
  179.3 7.4 %collective-permute-start.2 = (bf16[256,128]{1,0:T(8,128)(2,1)S(1)}, bf16[256,128]{1,0:T(8,128)(2,1)S(1)}, u32[]{:S(2)}, u32[]{:S(2)}) collective-permute-start(bf16[256,128]{1,0:T(8,128)(2,1)S(1)} %slice_reduce_fusion), channel_id=1, source_target_pairs={{0,3},{1,4},{2,5},{3,6},{4,7},{5,0},{6,1},{7,2},{8,11},{9,12},{10,... | collective-permute-start | bytes 196616 | tf_op jit(solution)/shard_map/ppermute | solution.py:521
  180.1 6.6 %collective-permute-start.1 = (bf16[256,128]{1,0:T(8,128)(2,1)S(1)}, bf16[256,128]{1,0:T(8,128)(2,1)S(1)}, u32[]{:S(2)}, u32[]{:S(2)}) collective-permute-start(bf16[256,128]{1,0:T(8,128)(2,1)S(1)} %slice_reduce_fusion), channel_id=1, source_target_pairs={{0,2},{1,3},{2,4},{3,5},{4,6},{5,7},{6,0},{7,1},{8,10},{9,11},{10,... | collective-permute-start | bytes 196616 | tf_op jit(solution)/shard_map/ppermute | solution.py:521
  181.3 6.6 %collective-permute-start = (bf16[256,128]{1,0:T(8,128)(2,1)S(1)}, bf16[256,128]{1,0:T(8,128)(2,1)S(1)}, u32[]{:S(2)}, u32[]{:S(2)}) collective-permute-start(bf16[256,128]{1,0:T(8,128)(2,1)S(1)} %slice_reduce_fusion), channel_id=1, source_target_pairs={{0,1},{1,2},{2,3},{3,4},{4,5},{5,6},{6,7},{7,0},{8,9},{9,10},{10,1... | collective-permute-start | bytes 196616 | tf_op jit(solution)/shard_map/ppermute | solution.py:521
  196.1 18.9 %all-to-all-start.5 = ((bf16[16,256,128]{2,1,0:T(8,128)(2,1)}), bf16[16,256,128]{2,1,0:T(8,128)(2,1)S(1)}, u32[]{:S(2)}, u32[]{:S(2)}) async-start(bf16[16,256,128]{2,1,0:T(8,128)(2,1)} %broadcast_in_dim.38), calls=%async_computation.5 | async-start | bytes 2097152 | tf_op jit(solution)/shard_map/all_to_all | solution.py:514
  215.0 1.0 copy-start.2

commit v5 on v4

--- a/solution.py
+++ b/solution.py
@@ -26,8 +26,7 @@
 SUM_ROWS = 16
 ROWS = BT // CHUNKS
 QUERY_ROWS = TILES_DEV * 64
-LIST_ROW = BT + QUERY_ROWS
-SEND_ROWS = LIST_ROW + 16
+SEND_ROWS = BT + QUERY_ROWS
 DW_ROWS = HW * D // 16 // 128
 MID_ROWS = ROWS + DW_ROWS
 END_ROWS = QUERY_ROWS + ROWS
@@ -59,11 +58,7 @@
 SMEM = pl.BlockSpec(memory_space=pltpu.SMEM)
 
 
-def pack_body(q_ref, k_ref, v_ref, list_ref, count_ref, out_ref, rows_ref):
-    rows_ref[...] = jnp.zeros(rows_ref.shape, F32)
-    rows_ref[:TILES_DEV, :MAXB] = list_ref[...].astype(F32)
-    rows_ref[8:9, :TILES_DEV] = count_ref[...].astype(F32)
-    lists = rows_ref[...].astype(BF16)
+def pack_body(q_ref, k_ref, v_ref, out_ref):
     kt = k_ref[...].T
     vt = v_ref[...].T
     qt = (q_ref[...].astype(F32) * SCALE).astype(BF16).T
@@ -71,7 +66,6 @@
         rows = slice(head * 64, head * 64 + 64)
         for half in range(2):
             dest = 2 * head + half
-            out_ref[dest, LIST_ROW:SEND_ROWS, :] = lists
             for j in range(4):
                 lanes = slice(j * 128, j * 128 + 128)
                 out_ref[dest, j * 128 : j * 128 + 64, :] = kt[rows, lanes]
@@ -81,7 +75,7 @@
                 out_ref[dest, BT + t * 64 : BT + t * 64 + 64, :] = qt[rows, low : low + HALF]
 
 
-def pack(q, k, v, lists, counts):
+def pack(q, k, v):
     return pl.pallas_call(
         pack_body,
         grid=(4,),
@@ -89,16 +83,13 @@
             pl.BlockSpec((TILES_DEV * QROWS, 128), lambda p: (0, p)),
             pl.BlockSpec((BT, 128), lambda p: (0, p)),
             pl.BlockSpec((BT, 128), lambda p: (0, p)),
-            pl.BlockSpec((TILES_DEV, MAXB), lambda p: (0, 0)),
-            pl.BlockSpec((1, TILES_DEV), lambda p: (0, 0)),
         ],
         out_specs=pl.BlockSpec((4, SEND_ROWS, 128), lambda p: (p, 0, 0)),
         out_shape=jax.ShapeDtypeStruct((16, SEND_ROWS, 128), BF16),
-        scratch_shapes=[pltpu.VMEM((16, 128), F32)],
         compiler_params=params(60),
         cost_estimate=cost(0, 8e6),
         name="pack",
-    )(q, k, v, lists, counts)
+    )(q, k, v)
 
 
 def dattn_body(w_ref, g_ref, out_ref):
@@ -129,7 +120,7 @@
     )(w, g)
 
 
-def plan_of(lists, counts):
+def plan_of(lists, counts, tiles):
     slots = jnp.arange(MAXB)[None, :] < counts[:, None]
     member = (
         (lists[:, :, None] == jnp.arange(BANDS)[None, None, :]) & slots[:, :, None]
@@ -140,7 +131,7 @@
     base = jnp.cumsum(size) - size
     flat = jnp.where(member > 0, 2 * base[:, None] + place, -1)
     hit = flat[None] == jnp.arange(2 * PAIRS)[:, None, None]
-    tile = jnp.arange(TILES)[None, None, :]
+    tile = tiles[None, None, :]
     band = jnp.arange(BANDS)[None, :, None]
     code = jnp.sum(jnp.where(hit, band * 64 + tile + 1, 0), axis=(1, 2)).reshape(PAIRS, 2)
     who = jnp.where(code > 0, (code & 63) - 1, TILES)
@@ -150,17 +141,36 @@
     ).astype(jnp.int32)
 
 
+def gather_lists(mine):
+    size = lax.axis_size("region")
+    step, rows = 1, mine
+    while step < size:
+        other = lax.ppermute(rows, "region", [((i + step) % size, i) for i in range(size)])
+        rows = jnp.concatenate([rows, other], axis=0)
+        step *= 2
+    tiles = (jnp.arange(TILES) + lax.axis_index("region") * TILES_DEV) % TILES
+    return rows, tiles
+
+
+def batched(count, width, body):
+    def step(j, carry):
+        for k in range(width):
+            body(j * width + k)
+        return carry
+
+    lax.fori_loop(0, count // width, step, 0)
+
+
 def forward_body(plan, recv, attn_ref, lse_ref, kv_ref, kt_ref, qt_ref, vt, top, acc, s0, s1, p0, p1, h0, h1):
-    def unpack_band(b, carry):
+    def unpack_band(b):
         kvt = jnp.concatenate([recv[b, j * 128 : j * 128 + 128, :] for j in range(4)], axis=1)
         kv_ref[b] = kvt.T
         kt_ref[b] = kvt[:64]
         vt[b] = jnp.concatenate([kvt[64:], jnp.ones((SUM_ROWS, BT), BF16)], axis=0)
         for t in range(TILES_DEV):
             qt_ref[b * TILES_DEV + t] = recv[b, BT + t * 64 : BT + t * 64 + 64, :]
-        return carry
-
-    lax.fori_loop(0, BANDS, unpack_band, 0)
+
+    batched(BANDS, 4, unpack_band)
     qt_ref[TILES] = jnp.zeros((64, HALF), BF16)
     top[...] = jnp.full(top.shape, LOW, F32)
     acc[...] = jnp.zeros(acc.shape, F32)
@@ -210,13 +220,12 @@
 
     lax.fori_loop(0, (plan[3, 0] + UNROLL - 1) // UNROLL, step, 0)
 
-    def finish(x, carry):
+    def finish(x):
         total = acc[x, 64:65, :]
-        attn_ref[x] = (acc[x, :64, :] / total).astype(BF16)
+        attn_ref[x] = (acc[x, :64, :] * (1.0 / total)).astype(BF16)
         lse_ref[x] = top[x] + jnp.log(total)
-        return carry
-
-    lax.fori_loop(0, TILES, finish, 0)
+
+    batched(TILES, 8, finish)
     lse_ref[TILES] = jnp.full((1, HALF), -LOW, F32)
 
 
@@ -256,16 +265,13 @@
     )(plan, recv)
 
 
-def backward_body(last, plan, kv, kt, qt, dot_, attn, lse, dq_in, send_ref, dq_ref, gt, delta, dkv, dq, s0, t0, s1, t1, p0, d0, p1, d1):
+def backward_body(last, plan, kv, kt, qt, dot_, attn, lse, dq_in, send_ref, dq_ref, delta, dkv, dq, s0, t0, s1, t1, p0, d0, p1, d1):
     rows = kv.shape[1]
 
-    def prepare(x, carry):
-        gt[x] = dot_[x]
+    def prepare(x):
         delta[x] = jnp.sum(attn[x].astype(F32) * dot_[x].astype(F32), axis=0, keepdims=True)
-        return carry
-
-    lax.fori_loop(0, TILES, prepare, 0)
-    gt[TILES] = jnp.zeros((64, HALF), BF16)
+
+    batched(TILES, 8, prepare)
     delta[TILES] = jnp.zeros((1, HALF), F32)
     dkv[...] = jnp.zeros(dkv.shape, F32)
     if dq_in is None:
@@ -277,9 +283,13 @@
     def pair(ref, i):
         return jnp.concatenate([ref[plan[0, i]], ref[plan[1, i]]], axis=1)
 
+    def pair_g(i):
+        a, c = jnp.minimum(plan[0, i], TILES - 1), jnp.minimum(plan[1, i], TILES - 1)
+        return jnp.concatenate([dot_[a], dot_[c]], axis=1)
+
     def scores(i, s, t, weigh=None):
         wq = jnp.concatenate([pair(qt, i), blank], axis=0)
-        wg = jnp.concatenate([blank, pair(gt, i)], axis=0)
+        wg = jnp.concatenate([blank, pair_g(i)], axis=0)
         for low in range(0, rows, BACK_SUB):
             at = slice(low, low + BACK_SUB)
             band = kv[plan[2, i], at, :]
@@ -299,7 +309,7 @@
         dq[a] += part[:, :HALF]
         dq[c] += part[:, HALF:]
         dkv[b, :64, :] += dot(pair(qt, i), d_ref[...], NT)
-        dkv[b, 64:, :] += dot(pair(gt, i), p_ref[...], NT)
+        dkv[b, 64:, :] += dot(pair_g(i), p_ref[...], NT)
 
     scores(0, s0, t0)
     scores(1, s1, t1)
@@ -319,16 +329,15 @@
 
     first = QUERY_ROWS if last else 0
 
-    def finish(b, carry):
+    def finish(b):
         for j in range(rows // 128):
             at = first + j * 128
             send_ref[b, at : at + 128, :] = dkv[b, :, j * 128 : j * 128 + 128].astype(BF16)
         if last:
             for t in range(TILES_DEV):
                 send_ref[b, t * 64 : t * 64 + 64, :] = (dq[b * TILES_DEV + t] * SCALE).astype(BF16)
-        return carry
-
-    lax.fori_loop(0, BANDS, finish, 0)
+
+    batched(BANDS, 4, finish)
     if not last:
         dq_ref[...] = dq[...]
 
@@ -372,7 +381,6 @@
         out_specs=out_specs,
         out_shape=out_shape,
         scratch_shapes=[
-            pltpu.VMEM((TILES + 1, 64, HALF), BF16),
             pltpu.VMEM((TILES + 1, 1, HALF), F32),
             pltpu.VMEM((BANDS, 128, ROWS), F32),
             pltpu.VMEM((TILES + 1, 64, HALF), F32),
@@ -400,21 +408,24 @@
         total = term if t == 0 else total + term
     total = total.astype(BF16)
     for dest in range(16):
-        send_ref[dest] = total[dest * 32 : dest * 32 + 32]
+        for j in range(4):
+            send_ref[dest, j * 32 : j * 32 + 32, :] = total[
+                dest * 32 : dest * 32 + 32, j * 128 : j * 128 + 128
+            ]
 
 
 def weight_grad(recv, g, send):
     rows = TILES_DEV * QROWS
-    steps = D // 128
+    steps = D // 512
     return pl.pallas_call(
         weight_body,
         grid=(steps,),
         in_specs=[
             pl.BlockSpec((16, QUERY_ROWS, 128), lambda j: (0, 0, 0)),
-            pl.BlockSpec((rows, 128), lambda j: (0, j)),
+            pl.BlockSpec((rows, 512), lambda j: (0, j)),
             pl.BlockSpec(memory_space=pl.ANY),
         ],
-        out_specs=pl.BlockSpec((16, 32, 128), lambda j: (0, ROWS // 32 + j, 0)),
+        out_specs=pl.BlockSpec((16, 128, 128), lambda j: (0, ROWS // 128 + j, 0)),
         out_shape=jax.ShapeDtypeStruct((BANDS, MID_ROWS, 128), BF16),
         input_output_aliases={2: 0},
         compiler_params=params(60),
@@ -464,27 +475,6 @@
             dv_ref[at, :] = jnp.concatenate([x[64:], y[64:]], axis=0).astype(BF16).T
 
 
-def weight_out_body(part, dw_ref):
-    for r in range(4):
-        for j in range(D // 128):
-            dw_ref[r * 32 : r * 32 + 32, j * 128 : j * 128 + 128] = part[
-                r, j * 32 : j * 32 + 32, :
-            ].astype(F32)
-
-
-def weight_out(part):
-    return pl.pallas_call(
-        weight_out_body,
-        grid=(4,),
-        in_specs=[pl.BlockSpec((4, DW_ROWS, 128), lambda p: (p, 0, 0))],
-        out_specs=pl.BlockSpec((128, D), lambda p: (p, 0)),
-        out_shape=jax.ShapeDtypeStruct((HW, D), F32),
-        compiler_params=params(60),
-        cost_estimate=cost(0, 3e6),
-        name="weight_out",
-    )(part)
-
-
 def unpack(mid, end):
     rows = TILES_DEV * QROWS
     return pl.pallas_call(
@@ -525,13 +515,14 @@
 def per_device(queries, keys, values, block_lists, band_counts, cotangent, out_weight):
     rows = TILES_DEV * QROWS
     q, g = queries.reshape(rows, HW), cotangent.reshape(rows, D)
-    k, v = keys.reshape(BT, HW), values.reshape(BT, HW)
-    recv = swap(pack(q, k, v, block_lists[0], band_counts))
-    lists = recv[:, LIST_ROW : LIST_ROW + TILES_DEV, :MAXB].astype(jnp.int32).reshape(TILES, MAXB)
-    counts = recv[:, LIST_ROW + 8, :TILES_DEV].astype(jnp.int32).reshape(TILES)
-    plan = plan_of(lists, counts)
+    packed = pack(q, keys.reshape(BT, HW), values.reshape(BT, HW))
+    lists = jnp.concatenate([block_lists[0], band_counts[0][:, None]], axis=1)
+    packed, lists = lax.optimization_barrier((packed, lists))
+    recv = swap(packed)
+    lists, tiles = gather_lists(lists)
+    plan = plan_of(lists[:, :MAXB], lists[:, MAXB], tiles)
     d_attn = dattn(out_weight, g)
-    recv, d_attn = lax.optimization_barrier((recv, d_attn))
+    recv, d_attn, plan = lax.optimization_barrier((recv, d_attn, plan))
     d_attn = swap(d_attn).reshape(TILES, 64, HALF)
 
     attn, lse, kv, kt, qt = forward(plan, recv)
@@ -546,16 +537,18 @@
     end = swap(end)
     share = jnp.sum(mid[:, ROWS:].astype(F32), axis=0).astype(BF16)
     total = orbit_sum(share).astype(BF16)
+    total = total.reshape(D // 128, 32, 128).transpose(1, 0, 2).reshape(1, 32, D)
+    total = jnp.broadcast_to(total, (16, 32, D))
     layer = layer_output(attn_home, out_weight)
     end, total, layer = lax.optimization_barrier((end, total, layer))
-    total = swap(jnp.broadcast_to(total[None], (16, DW_ROWS, 128)))
+    total = swap(total)
     d_q, d_k, d_v = unpack(mid, end)
     return (
         layer.reshape(1, TILES_DEV, QROWS, D),
         d_q.reshape(1, TILES_DEV, QROWS, HW),
         d_k.reshape(1, 1, BT, HW),
         d_v.reshape(1, 1, BT, HW),
-        weight_out(total),
+        total.reshape(HW, D).astype(F32),
     )
 
 

time: 221 us -> 225 us (1.018)
  starting transfers between devices: 48.4 us -> 64.7 us
  Pallas kernels: 105 us -> 96 us
  waiting for transfers between devices: 57 us -> 51.5 us
    all_to_all x6, waiting for transfers between devices: 55.3 us -> 15.1 us  [swap(): return lax.all_to_all(x, axes, 0, 0, tiled=True)]
    ppermute x0 -> x4, waiting for transfers between devices: none -> 34.4 us  [gather_lists(): lax.ppermute(rows, 'region', [((i + step) % size, i) for i in range(size)])]
    ppermute x0 -> x4, starting transfers between devices: none -> 14.4 us  [gather_lists(): lax.ppermute(rows, 'region', [((i + step) % size, i) for i in range(size)])]
    all_to_all x6, starting transfers between devices: 38 us -> 42.5 us  [swap(): return lax.all_to_all(x, axes, 0, 0, tiled=True)]
    pallas_call x1, Pallas kernels: 7.05 us -> 3.37 us  [weight_grad(): pl.pallas_call(weight_body, grid=(steps,), in_specs=[pl.BlockSpec((16, QU...]
    pallas_call x1 -> x0, Pallas kernels: 3.57 us -> none  [weight_out(): pl.pallas_call(weight_out_body, grid=(4,), in_specs=[pl.BlockSpec((4, DW_...]
    ppermute x7, starting transfers between devices: 10.4 us -> 7.78 us  [orbit_sum(): lax.ppermute(share, 'orbit', [(i, (i + shift) % size) for i in range(size)])]
  transfers between devices with their start and end apart: 13 -> 17, of which waited for: 6 -> 8; matrix products, arithmetic and copies ran while one was open for 1% -> 2% of each run, Pallas kernels for 41% -> 40%
where the time goes in v5:
time: 225 us; the launch traced here: 222 us
  Pallas kernels  96 us (43%)
  starting transfers between devices  64.7 us (29%)
  waiting for transfers between devices  51.5 us (23%)
  local copies, waits for them, and re-layouts  5.12 us (2%)
  other arithmetic  4.28 us (2%)
    pallas_call x2, Pallas kernels, backward(): pl.pallas_call(body, grid=(1,), in_specs=specs, out_specs=out_specs, out_...  50.3 us
    all_to_all x6, starting transfers between devices, swap(): return lax.all_to_all(x, axes, 0, 0, tiled=True)  42.5 us
    ppermute x4, waiting for transfers between devices, gather_lists(): lax.ppermute(rows, 'region', [((i + step) % size, i) for i in range(size)])  34.4 us
    pallas_call x1, Pallas kernels, forward(): pl.pallas_call(forward_body, grid=(1,), in_specs=[SMEM, whole(16, SEND_RO...  24.9 us
    all_to_all x6, waiting for transfers between devices, swap(): return lax.all_to_all(x, axes, 0, 0, tiled=True)  15.1 us
    ppermute x4, starting transfers between devices, gather_lists(): lax.ppermute(rows, 'region', [((i + step) % size, i) for i in range(size)])  14.4 us
    ppermute x7, starting transfers between devices, orbit_sum(): lax.ppermute(share, 'orbit', [(i, (i + shift) % size) for i in range(size)])  7.78 us
    pallas_call x1, Pallas kernels, dattn(): pl.pallas_call(dattn_body, grid=(4,), in_specs=[pl.BlockSpec((128, D), la...  5.18 us
  transfers between devices with their start and end apart: 17, of which 8 were waited for; matrix products, arithmetic and copies ran while one was open for 2% of the time, Pallas kernels for 40%

profile of v5, /device:TPU:0, one launch (start us, length us, event | category | flops | bytes accessed | tf_op | source)
XLA Modules:
  0.0 222.4 jit_solution(15005914067993725377)
XLA Ops:
  2.1 4.2 %pack.1 = bf16[16,704,128]{2,1,0:T(8,128)(2,1)} custom-call(bf16[768,512]{1,0:T(8,128)(2,1)} %bitcast.45, bf16[512,512]{1,0:T(8,128)(2,1)} %bitcast.47, bf16[512,512]{1,0:T(8,128)(2,1)} %bitcast.48), custom_call_target="tpu_custom_call" | custom-call | bytes 8000000 | tf_op jit(solution)/shard_map/pack/pallas_call | solution.py:79
  6.4 8.0 %all-to-all-start = ((bf16[16,704,128]{2,1,0:T(8,128)(2,1)}), bf16[16,704,128]{2,1,0:T(8,128)(2,1)S(1)}, u32[]{:S(2)}, u32[]{:S(2)}) async-start(bf16[16,704,128]{2,1,0:T(8,128)(2,1)} %pack.1), calls=%async_computation | async-start | bytes 5767168 | tf_op jit(solution)/shard_map/all_to_all | solution.py:504
  14.3 5.3 %collective-permute-start = (s32[3,9]{1,0:T(4,128)S(1)}, s32[3,9]{1,0:T(4,128)S(1)}, u32[]{:S(2)}, u32[]{:S(2)}) collective-permute-start(s32[3,9]{1,0:T(4,128)S(1)} %pad_add_fusion.3), channel_id=1, source_target_pairs={{8,0},{16,8},{24,16},{32,24},{40,32},{48,40},{56,48},{64,56},{72,6... | collective-permute-start | bytes 332 | tf_op jit(solution)/shard_map/ppermute | solution.py:148
  19.6 27.6 %collective-permute-done = s32[3,9]{1,0:T(4,128)S(1)} collective-permute-done((s32[3,9]{1,0:T(4,128)S(1)}, s32[3,9]{1,0:T(4,128)S(1)}, u32[]{:S(2)}, u32[]{:S(2)}) %collective-permute-start) | collective-permute-done | bytes 140 | tf_op jit(solution)/shard_map/ppermute | solution.py:148
  47.2 5.4 %collective-permute-done.1 = s32[6,9]{1,0:T(8,128)S(1)} collective-permute-done((s32[6,9]{1,0:T(8,128)S(1)}, s32[6,9]{1,0:T(8,128)S(1)}, u32[]{:S(2)}, u32[]{:S(2)}) %collective-permute-start.1) | collective-permute-done | bytes 248 | tf_op jit(solution)/shard_map/ppermute | solution.py:148
  52.7 7.4 %collective-permute-start.2 = (s32[12,9]{1,0:T(8,128)S(1)}, s32[12,9]{1,0:T(8,128)S(1)}, u32[]{:S(2)}, u32[]{:S(2)}) collective-permute-start(s32[12,9]{1,0:T(8,128)S(1)} %pad_add_fusion.1), channel_id=1, source_target_pairs={{32,0},{40,8},{48,16},{56,24},{64,32},{72,40},{80,48},{88,56},{96,... | collective-permute-start | bytes 1304 | tf_op jit(solution)/shard_map/ppermute | solution.py:148
  61.4 1.8 collective-permute-start.3
  63.2 5.2 %dattn.1 = bf16[16,192,128]{2,1,0:T(8,128)(2,1)} custom-call(bf16[512,1024]{1,0:T(8,128)(2,1)} %w_ref.3, bf16[768,1024]{1,0:T(8,128)(2,1)} %bitcast.42), custom_call_target="tpu_custom_call" | custom-call | flops 805306368 | bytes 4000000 | tf_op jit(solution)/shard_map/dattn/pallas_call | solution.py:108
  72.5 7.5 %all-to-all-start.2 = ((bf16[16,192,128]{2,1,0:T(8,128)(2,1)}), bf16[16,192,128]{2,1,0:T(8,128)(2,1)}, u32[]{:S(2)}, u32[]{:S(2)}) async-start(bf16[16,192,128]{2,1,0:T(8,128)(2,1)} %dattn.1), calls=%async_computation.2 | async-start | bytes 1572864 | tf_op jit(solution)/shard_map/all_to_all | solution.py:504
  80.0 24.9 %forward.1 = (bf16[48,64,128]{2,1,0:T(8,128)(2,1)}, f32[49,1,128]{2,1,0:T(1,128)}, bf16[16,512,128]{2,1,0:T(8,128)(2,1)}, bf16[16,64,512]{2,1,0:T(8,128)(2,1)}, bf16[49,64,128]{2,1,0:T(8,128)(2,1)}) custom-call(s32[4,208]{1,0:T(4,128)} %add_add_fusion.1.plan.refs_0_, bf16[16,704,128]{2,1,0:T(8,128)(2,1)} %copy-done.2), custom_call_target="tpu_custom_call" | custom-call | flops 24000000000 | bytes 20000000 | tf_op jit(solution)/shard_map/forward/pallas_call | solution.py:233
  105.0 7.2 %all-to-all-start.1 = ((bf16[16,192,128]{2,1,0:T(8,128)(2,1)}), bf16[16,192,128]{2,1,0:T(8,128)(2,1)S(1)}, u32[]{:S(2)}, u32[]{:S(2)}) async-start(bf16[16,192,128]{2,1,0:T(8,128)(2,1)} %bitcast.46), calls=%async_computation.1 | async-start | bytes 1572864 | tf_op jit(solution)/shard_map/all_to_all | solution.py:504
  112.2 25.0 %backward.2 = (bf16[16,512,128]{2,1,0:T(8,128)(2,1)}, f32[49,64,128]{2,1,0:T(8,128)}) custom-call(s32[4,208]{1,0:T(4,128)} %add_add_fusion.1.plan.refs_0_, bf16[16,512,128]{2,1,0:T(8,128)(2,1)} %get-tuple-element.35.refs_1_, bf16[16,64,512]{2,1,0:T(8,128)(2,1)} %get-tuple-element.36.refs_2_, bf16[49,64,128]{2,1,0:T(8,128)(2,1)} %get-tuple-element.37.refs_3_, ...), custom_call_target="tpu_custom_call" | custom-call | flops 24999999488 | bytes 20000000 | tf_op jit(solution)/shard_map/backward/pallas_call | solution.py:377
  138.0 3.4 %weight_grad.1 = bf16[16,512,128]{2,1,0:T(8,128)(2,1)} custom-call(bf16[16,192,128]{2,1,0:T(8,128)(2,1)} %copy-done.1, bf16[768,1024]{1,0:T(8,128)(2,1)} %bitcast.43, bf16[16,512,128]{2,1,0:T(8,128)(2,1)} %get-tuple-element.42.unused), custom_call_target="tpu_custom_call", output_to_operand_aliasing={{}: (2, {})} | custom-call | flops 805306368 | bytes 5000000 | tf_op jit(solution)/shard_map/weight_grad/pallas_call | solution.py:420
  141.4 7.2 %all-to-all-start.3 = ((bf16[16,512,128]{2,1,0:T(8,128)(2,1)}), bf16[16,512,128]{2,1,0:T(8,128)(2,1)S(1)}, u32[]{:S(2)}, u32[]{:S(2)}) async-start(bf16[16,512,128]{2,1,0:T(8,128)(2,1)} %weight_grad.1), calls=%async_computation.3 | async-start | bytes 4194304 | tf_op jit(solution)/shard_map/all_to_all | solution.py:504
  148.6 25.3 %backward.3 = bf16[16,448,128]{2,1,0:T(8,128)(2,1)} custom-call(s32[4,208]{1,0:T(4,128)} %add_add_fusion.1.plan.refs_0_, bf16[16,512,128]{2,1,0:T(8,128)(2,1)} %get-tuple-element.35.refs_1_, bf16[16,64,512]{2,1,0:T(8,128)(2,1)} %get-tuple-element.36.refs_2_, bf16[49,64,128]{2,1,0:T(8,128)(2,1)} %get-tuple-element.37.refs_3_, ...), custom_call_target="tpu_custom_call" | custom-call | flops 24999999488 | bytes 20000000 | tf_op jit(solution)/shard_map/backward/pallas_call | solution.py:377
  173.9 7.3 %all-to-all-start.4 = ((bf16[16,448,128]{2,1,0:T(8,128)(2,1)}), bf16[16,448,128]{2,1,0:T(8,128)(2,1)}, u32[]{:S(2)}, u32[]{:S(2)}) async-start(bf16[16,448,128]{2,1,0:T(8,128)(2,1)} %backward.3), calls=%async_computation.4 | async-start | bytes 3670016 | tf_op jit(solution)/shard_map/all_to_all | solution.py:504
  181.4 3.2 %collective-permute-start.9 = (bf16[256,128]{1,0:T(8,128)(2,1)S(1)}, bf16[256,128]{1,0:T(8,128)(2,1)S(1)}, u32[]{:S(2)}, u32[]{:S(2)}) collective-permute-start(bf16[256,128]{1,0:T(8,128)(2,1)S(1)} %slice_reduce_fusion), channel_id=1, source_target_pairs={{0,6},{1,7},{2,0},{3,1},{4,2},{5,3},{6,4},{7,5},{8,14},{9,15},{10,... | collective-permute-start | bytes 196616 | tf_op jit(solution)/shard_map/ppermute | solution.py:511
  185.0 2.9 %collective-permute-start.7 = (bf16[256,128]{1,0:T(8,128)(2,1)S(1)}, bf16[256,128]{1,0:T(8,128)(2,1)S(1)}, u32[]{:S(2)}, u32[]{:S(2)}) collective-permute-start(bf16[256,128]{1,0:T(8,128)(2,1)S(1)} %slice_reduce_fusion), channel_id=1, source_target_pairs={{0,4},{1,5},{2,6},{3,7},{4,0},{5,1},{6,2},{7,3},{8,12},{9,13},{10,... | collective-permute-start | bytes 196616 | tf_op jit(solution)/shard_map/ppermute | solution.py:511
  189.1 4.0 %layer_output.1 = bf16[768,1024]{1,0:T(8,128)(2,1)} custom-call(bf16[16,192,128]{2,1,0:T(8,128)(2,1)} %copy-done.1, bf16[512,1024]{1,0:T(8,128)(2,1)} %w_ref.3), custom_call_target="tpu_custom_call" | custom-call | flops 805306368 | bytes 4000000 | tf_op jit(solution)/shard_map/layer_output/pallas_call | solution.py:444
  195.3 6.2 %all-to-all-done.4.end = bf16[16,448,128]{2,1,0:T(8,128)(2,1)} async-done(((bf16[16,448,128]{2,1,0:T(8,128)(2,1)}), bf16[16,448,128]{2,1,0:T(8,128)(2,1)}, u32[]{:S(2)}, u32[]{:S(2)}) %all-to-all-start.4) | async-done | bytes 1835040 | tf_op jit(solution)/shard_map/all_to_all | solution.py:504
  202.6 5.3 %all-to-all-start.5 = ((bf16[16,32,1024]{2,1,0:T(8,128)(2,1)}), bf16[16,32,1024]{2,1,0:T(8,128)(2,1)S(1)}, u32[]{:S(2)}, u32[]{:S(2)}) async-start(bf16[16,32,1024]{2,1,0:T(8,128)(2,1)} %broadcast_in_dim.41), calls=%async_computation.5 | async-start | bytes 2097152 | tf_op jit(solution)/shard_map/all_to_all | solution.py:504
  207.9 4.0 %unpack.1 = (bf16[768,512]{1,0:T(8,128)(2,1)}, bf16[512,512]{1,0:T(8,128)(2,1)}, bf16[512,512]{1,0:T(8,128)(2,1)}) custom-call(bf16[16,512,128]{2,1,0:T(8,128)(2,1)} %copy-done, bf16[16,448,128]{2,1,0:T(8,128)(2,1)} %all-to-all-done.4.end), custom_call_target="tpu_custom_call" | custom-call | bytes 8000000 | tf_op jit(solution)/shard_map/unpack/pallas_call | solution.py:480
  211.9 8.9 %all-to-all-done.5 = bf16[16,32,1024]{2,1,0:T(8,128)(2,1)S(1)} async-done(((bf16[16,32,1024]{2,1,0:T(8,128)(2,1)}), bf16[16,32,1024]{2,1,0:T(8,128)(2,1)S(1)}, u32[]{:S(2)}, u32[]{:S(2)}) %all-to-all-start.5) | async-done | bytes 1048608 | tf_op jit(solution)/shard_map/all_to_all | solution.py:504
  220.8 1.6 bitcast_convert_fusion
  (64 shorter events, 12.9 us)
Async XLA Ops:
  6.4 66.1 %all-to-all-start = ((bf16[16,704,128]{2,1,0:T(8,128)(2,1)}), bf16[16,704,128]{2,1,0:T(8,128)(2,1)S(1)}, u32[]{:S(2)}, u32[]{:S(2)}) async-start(bf16[16,704,128]{2,1,0:T(8,128)(2,1)} %pack.1), calls=%async_computation | async-start | bytes 5767168 | tf_op jit(solution)/shard_map/all_to_all | solution.py:504
  14.3 32.9 %collective-permute-start = (s32[3,9]{1,0:T(4,128)S(1)}, s32[3,9]{1,0:T(4,128)S(1)}, u32[]{:S(2)}, u32[]{:S(2)}) collective-permute-start(s32[3,9]{1,0:T(4,128)S(1)} %pad_add_fusion.3), channel_id=1, source_target_pairs={{8,0},{16,8},{24,16},{32,24},{40,32},{48,40},{56,48},{64,56},{72,6... | collective-permute-start | bytes 332 | tf_op jit(solution)/shard_map/ppermute | solution.py:148
  47.2 5.5 %collective-permute-start.1 = (s32[6,9]{1,0:T(8,128)S(1)}, s32[6,9]{1,0:T(8,128)S(1)}, u32[]{:S(2)}, u32[]{:S(2)}) collective-permute-start(s32[6,9]{1,0:T(8,128)S(1)} %pad_add_fusion.2), channel_id=1, source_target_pairs={{16,0},{24,8},{32,16},{40,24},{48,32},{56,40},{64,48},{72,56},{80,... | collective-permute-start | bytes 656 | tf_op jit(solution)/shard_map/ppermute | solution.py:148
  52.7 8.8 %collective-permute-start.2 = (s32[12,9]{1,0:T(8,128)S(1)}, s32[12,9]{1,0:T(8,128)S(1)}, u32[]{:S(2)}, u32[]{:S(2)}) collective-permute-start(s32[12,9]{1,0:T(8,128)S(1)} %pad_add_fusion.1), channel_id=1, source_target_pairs={{32,0},{40,8},{48,16},{56,24},{64,32},{72,40},{80,48},{88,56},{96,... | collective-permute-start | bytes 1304 | tf_op jit(solution)/shard_map/ppermute | solution.py:148
  61.4 7.4 %collective-permute-start.3 = (s32[24,9]{1,0:T(8,128)S(1)}, s32[24,9]{1,0:T(8,128)S(1)}, u32[]{:S(2)}, u32[]{:S(2)}) collective-permute-start(s32[24,9]{1,0:T(8,128)S(1)} %pad_add_fusion), channel_id=1, source_target_pairs={{64,0},{72,8},{80,16},{88,24},{96,32},{104,40},{112,48},{120,56},{... | collective-permute-start | bytes 2600 | tf_op jit(solution)/shard_map/ppermute | solution.py:148
  72.5 7.6 %copy-start.2 = (bf16[16,704,128]{2,1,0:T(8,128)(2,1)}, bf16[16,704,128]{2,1,0:T(8,128)(2,1)S(1)}, u32[]{:S(2)}) copy-start(bf16[16,704,128]{2,1,0:T(8,128)(2,1)S(1)} %all-to-all-done.recv) | copy-start | bytes 8650756
  72.5 32.5 %all-to-all-start.2 = ((bf16[16,192,128]{2,1,0:T(8,128)(2,1)}), bf16[16,192,128]{2,1,0:T(8,128)(2,1)}, u32[]{:S(2)}, u32[]{:S(2)}) async-start(bf16[16,192,128]{2,1,0:T(8,128)(2,1)} %dattn.1), calls=%async_computation.2 | async-start | bytes 1572864 | tf_op jit(solution)/shard_map/all_to_all | solution.py:504
  105.0 32.2 %all-to-all-start.1 = ((bf16[16,192,128]{2,1,0:T(8,128)(2,1)}), bf16[16,192,128]{2,1,0:T(8,128)(2,1)S(1)}, u32[]{:S(2)}, u32[]{:S(2)}) async-start(bf16[16,192,128]{2,1,0:T(8,128)(2,1)} %bitcast.46), calls=%async_computation.1 | async-start | bytes 1572864 | tf_op jit(solution)/shard_map/all_to_all | solution.py:504
  137.1 0.9 copy-start.1
  141.4 32.5 %all-to-all-start.3 = ((bf16[16,512,128]{2,1,0:T(8,128)(2,1)}), bf16[16,512,128]{2,1,0:T(8,128)(2,1)S(1)}, u32[]{:S(2)}, u32[]{:S(2)}) async-start(bf16[16,512,128]{2,1,0:T(8,128)(2,1)} %weight_grad.1), calls=%async_computation.3 | async-start | bytes 4194304 | tf_op jit(solution)/shard_map/all_to_all | solution.py:504
  173.9 7.3 %copy-start = (bf16[16,512,128]{2,1,0:T(8,128)(2,1)}, bf16[16,512,128]{2,1,0:T(8,128)(2,1)S(1)}, u32[]{:S(2)}) copy-start(bf16[16,512,128]{2,1,0:T(8,128)(2,1)S(1)} %all-to-all-done.3.mid) | copy-start | bytes 6291460
  173.9 27.5 %all-to-all-start.4 = ((bf16[16,448,128]{2,1,0:T(8,128)(2,1)}), bf16[16,448,128]{2,1,0:T(8,128)(2,1)}, u32[]{:S(2)}, u32[]{:S(2)}) async-start(bf16[16,448,128]{2,1,0:T(8,128)(2,1)} %backward.3), calls=%async_computation.4 | async-start | bytes 3670016 | tf_op jit(solution)/shard_map/all_to_all | solution.py:504
  181.3 6.5 %collective-permute-start.10 = (bf16[256,128]{1,0:T(8,128)(2,1)S(1)}, bf16[256,128]{1,0:T(8,128)(2,1)S(1)}, u32[]{:S(2)}, u32[]{:S(2)}) collective-permute-start(bf16[256,128]{1,0:T(8,128)(2,1)S(1)} %slice_reduce_fusion), channel_id=1, source_target_pairs={{0,7},{1,0},{2,1},{3,2},{4,3},{5,4},{6,5},{7,6},{8,15},{9,8},{10,9... | collective-permute-start | bytes 196616 | tf_op jit(solution)/shard_map/ppermute | solution.py:511
  181.4 6.7 %collective-permute-start.9 = (bf16[256,128]{1,0:T(8,128)(2,1)S(1)}, bf16[256,128]{1,0:T(8,128)(2,1)S(1)}, u32[]{:S(2)}, u32[]{:S(2)}) collective-permute-start(bf16[256,128]{1,0:T(8,128)(2,1)S(1)} %slice_reduce_fusion), channel_id=1, source_target_pairs={{0,6},{1,7},{2,0},{3,1},{4,2},{5,3},{6,4},{7,5},{8,14},{9,15},{10,... | collective-permute-start | bytes 196616 | tf_op jit(solution)/shard_map/ppermute | solution.py:511
  184.5 8.6 %collective-permute-start.8 = (bf16[256,128]{1,0:T(8,128)(2,1)S(1)}, bf16[256,128]{1,0:T(8,128)(2,1)S(1)}, u32[]{:S(2)}, u32[]{:S(2)}) collective-permute-start(bf16[256,128]{1,0:T(8,128)(2,1)S(1)} %slice_reduce_fusion), channel_id=1, source_target_pairs={{0,5},{1,6},{2,7},{3,0},{4,1},{5,2},{6,3},{7,4},{8,13},{9,14},{10,... | collective-permute-start | bytes 196616 | tf_op jit(solution)/shard_map/ppermute | solution.py:511
  185.0 8.2 %collective-permute-start.7 = (bf16[256,128]{1,0:T(8,128)(2,1)S(1)}, bf16[256,128]{1,0:T(8,128)(2,1)S(1)}, u32[]{:S(2)}, u32[]{:S(2)}) collective-permute-start(bf16[256,128]{1,0:T(8,128)(2,1)S(1)} %slice_reduce_fusion), channel_id=1, source_target_pairs={{0,4},{1,5},{2,6},{3,7},{4,0},{5,1},{6,2},{7,3},{8,12},{9,13},{10,... | collective-permute-start | bytes 196616 | tf_op jit(solution)/shard_map/ppermute | solution.py:511
  187.8 5.8 %collective-permute-start.6 = (bf16[256,128]{1,0:T(8,128)(2,1)S(1)}, bf16[256,128]{1,0:T(8,128)(2,1)S(1)}, u32[]{:S(2)}, u32[]{:S(2)}) collective-permute-start(bf16[256,128]{1,0:T(8,128)(2,1)S(1)} %slice_reduce_fusion), channel_id=1, source_target_pairs={{0,3},{1,4},{2,5},{3,6},{4,7},{5,0},{6,1},{7,2},{8,11},{9,12},{10,... | collective-permute-start | bytes 196616 | tf_op jit(solution)/shard_map/ppermute | solution.py:511
  187.8 6.7 %collective-permute-start.5 = (bf16[256,128]{1,0:T(8,128)(2,1)S(1)}, bf16[256,128]{1,0:T(8,128)(2,1)S(1)}, u32[]{:S(2)}, u32[]{:S(2)}) collective-permute-start(bf16[256,128]{1,0:T(8,128)(2,1)S(1)} %slice_reduce_fusion), channel_id=1, source_target_pairs={{0,2},{1,3},{2,4},{3,5},{4,6},{5,7},{6,0},{7,1},{8,10},{9,11},{10,... | collective-permute-start | bytes 196616 | tf_op jit(solution)/shard_map/ppermute | solution.py:511
  188.1 7.1 %collective-permute-start.4 = (bf16[256,128]{1,0:T(8,128)(2,1)S(1)}, bf16[256,128]{1,0:T(8,128)(2,1)S(1)}, u32[]{:S(2)}, u32[]{:S(2)}) collective-permute-start(bf16[256,128]{1,0:T(8,128)(2,1)S(1)} %slice_reduce_fusion), channel_id=1, source_target_pairs={{0,1},{1,2},{2,3},{3,4},{4,5},{5,6},{6,7},{7,0},{8,9},{9,10},{10,1... | collective-permute-start | bytes 196616 | tf_op jit(solution)/shard_map/ppermute | solution.py:511
  202.6 18.2 %all-to-all-start.5 = ((bf16[16,32,1024]{2,1,0:T(8,128)(2,1)}), bf16[16,32,1024]{2,1,0:T(8,128)(2,1)S(1)}, u32[]{:S(2)}, u32[]{:S(2)}) async-start(bf16[16,32,1024]{2,1,0:T(8,128)(2,1)} %broadcast_in_dim.41), calls=%async_computation.5 | async-start | bytes 2097152 | tf_op jit(solution)/shard_map/all_to_all | solution.py:504
